TPU v7x, 128 devices: a whole 4x4x4 slice. The times are simulated.
128 devices in a mesh: band: 8 (over y_hi, x), led: 4 (over z), pencil: 4 (over y_lo, core).
Axes of the slice: x: 4, y: 4 (y_hi: 2, y_lo: 2; y = y_hi * 2 + y_lo), z: 4, core: 2. Of those that a mesh axis runs over, the one named last changes fastest.
Arguments:
- spectrum: float32 [128, 64, 2, 8192], P(('band', 'led', 'pencil')), may hold values from -6 to 6
- pupil: float32 [2, 2048, 2048], P(None, None, ('band', 'pencil')), may hold values from -5 to 5
- measured: float32 [8, 2048, 2048], P('led', ('band', 'pencil')), may hold values from 0.05 to 4
- offsets: int32 [8, 2], replicated, may hold values from 0 to 6144
Outputs:
- spectrum_grad: float32 [128, 64, 2, 8192], P(('band', 'led', 'pencil'))
- pupil_grad: float32 [2, 2048, 2048], P(None, None, ('band', 'pencil'))
Inputs may be any that keep to these rules, and one draw needn't show every extreme that they name: offsets[l, 0] and offsets[l, 1] are the first row and first column of LED l's window, which lies inside the spectrum.
All inputs are finite; a program needn't handle non-finite values.
Results may differ from a plain program's by a relative error of at most 0.008.
Values may be sent and summed in bfloat16 or wider, within the bound.
A program may use at most 128 MiB of HBM per device.

v0:
```python
import math

import jax
import jax.numpy as jnp
from jax import lax
from jax.sharding import PartitionSpec as P


def make_tables(size):
    rows = lax.broadcasted_iota(jnp.int32, (size, size), 0)
    cols = lax.broadcasted_iota(jnp.int32, (size, size), 1)
    phase = (rows * cols % size).astype(jnp.float32) * (2.0 * math.pi / size)
    return (jnp.cos(phase).astype(jnp.bfloat16), jnp.sin(phase).astype(jnp.bfloat16))


def contract_first(left, right):
    return lax.dot_general(
        left, right, (((0,), (0,)), ((), ())), preferred_element_type=jnp.float32
    )


def local(spectrum, pupil, measured, offsets):
    local_rows = spectrum[0]
    extent = local_rows.shape[2]
    window = pupil.shape[1]
    pencil_cols = pupil.shape[2]
    per_group = measured.shape[0]
    groups = lax.axis_size("led")
    band_count = lax.axis_size("band")
    pencils = lax.axis_size("pencil")
    col_blocks = band_count * pencils
    devices = band_count * groups * pencils
    strips = window // devices
    led_count = groups * per_group
    device_id = lax.axis_index(("band", "led", "pencil"))
    group_id = lax.axis_index("led")
    row_start = offsets[:, 0]
    col_start = offsets[:, 1]
    zero_index = jnp.int32(0)
    first_row = (row_start - device_id + devices - 1) // devices
    pieces = jnp.stack(
        [
            lax.dynamic_slice(
                local_rows, (first_row[led_id], zero_index, col_start[led_id]), (strips, 2, window)
            )
            for led_id in range(led_count)
        ]
    ).astype(jnp.bfloat16)
    mine_rows = lax.dynamic_slice_in_dim(row_start, group_id * per_group, per_group)
    natural = lax.broadcasted_iota(jnp.int32, (per_group, window), 1)
    global_row = mine_rows[:, None] + natural
    src_dev = global_row % devices
    src_local = global_row // devices - (mine_rows[:, None] - src_dev + devices - 1) // devices
    concat_pos = lax.broadcasted_iota(jnp.int32, (per_group, window), 1)
    outgoing = (
        pieces.reshape(groups, per_group, strips, 2, col_blocks, pencil_cols)
        .transpose(0, 1, 2, 4, 3, 5)
        .reshape(groups, per_group, strips, col_blocks, 2 * pencil_cols)
    )
    received = lax.all_to_all(
        lax.all_to_all(outgoing, ("band", "pencil"), split_axis=3, concat_axis=2, tiled=True),
        "led",
        split_axis=0,
        concat_axis=2,
        tiled=True,
    )
    src_band = src_dev // (groups * pencils)
    src_group = src_dev // pencils % groups
    src_pencil = src_dev % pencils
    position = (src_group * col_blocks + src_band * pencils + src_pencil) * strips + src_local
    pos_group = concat_pos // (col_blocks * strips)
    pos_block = concat_pos // strips % col_blocks
    pos_local = concat_pos % strips
    pos_device = (pos_block // pencils * groups + pos_group) * pencils + pos_block % pencils
    pos_first = (mine_rows[:, None] - pos_device + devices - 1) // devices
    anchor = (pos_first + pos_local) * devices + pos_device - mine_rows[:, None]
    windows = jnp.take_along_axis(
        received.reshape(per_group, window, 2 * pencil_cols), position[:, :, None], axis=1
    )
    cosine, sine_table = make_tables(window)
    pupil_re = pupil[0]
    pupil_im = pupil[1]
    halves = []
    for member in range(per_group):
        win = windows[member].reshape(window, 2, pencil_cols)
        win_re = win[:, 0, :]
        win_im = win[:, 1, :]
        prod_re = win_re * pupil_re - win_im * pupil_im
        prod_im = win_re * pupil_im + win_im * pupil_re
        product = (
            jnp.stack([prod_re, prod_im], axis=1)
            .astype(jnp.bfloat16)
            .reshape(window, 2 * pencil_cols)
        )
        with_cos = contract_first(product, cosine).reshape(2, pencil_cols, window)
        with_sin = contract_first(product, sine_table).reshape(2, pencil_cols, window)
        half_re = (with_cos[0] - with_sin[1]).reshape(pencil_cols, col_blocks, pencil_cols)
        half_im = (with_cos[1] + with_sin[0]).reshape(pencil_cols, col_blocks, pencil_cols)
        halves.append(
            jnp.stack([half_re, half_im], axis=2)
            .astype(jnp.bfloat16)
            .reshape(pencil_cols, col_blocks, 2 * pencil_cols)
        )
    half_all = jnp.stack(halves)
    row_side = lax.all_to_all(
        half_all, ("band", "pencil"), split_axis=2, concat_axis=1, tiled=True
    ).reshape(per_group, window, 2 * pencil_cols)
    back_list = []
    for member in range(per_group):
        with_cos = contract_first(row_side[member], cosine).reshape(2, pencil_cols, window)
        with_sin = contract_first(row_side[member], sine_table).reshape(2, pencil_cols, window)
        field_re = (with_cos[0] - with_sin[1]) / window
        field_im = (with_cos[1] + with_sin[0]) / window
        amplitude = jnp.sqrt(field_re * field_re + field_im * field_im)
        factor = 1.0 - jnp.sqrt(measured[member]) / jnp.maximum(amplitude, 0.5)
        residual = (
            jnp.stack([field_re * factor, field_im * factor])
            .astype(jnp.bfloat16)
            .reshape(2 * pencil_cols, window)
        )
        back_cos = jnp.dot(residual, cosine, preferred_element_type=jnp.float32).reshape(
            2, pencil_cols, window
        )
        back_sin = jnp.dot(residual, sine_table, preferred_element_type=jnp.float32).reshape(
            2, pencil_cols, window
        )
        back_re = (back_cos[0] + back_sin[1]).reshape(pencil_cols, col_blocks, pencil_cols)
        back_im = (back_cos[1] - back_sin[0]).reshape(pencil_cols, col_blocks, pencil_cols)
        back_list.append(
            jnp.stack([back_re, back_im], axis=2)
            .astype(jnp.bfloat16)
            .reshape(pencil_cols, col_blocks, 2 * pencil_cols)
        )
    back_all = jnp.stack(back_list)
    col_side = lax.all_to_all(
        back_all, ("band", "pencil"), split_axis=2, concat_axis=1, tiled=True
    ).reshape(per_group, window, 2 * pencil_cols)
    terms = []
    pupil_total = jnp.zeros((2, window, pencil_cols), jnp.float32)
    for member in range(per_group):
        grad_cos = contract_first(cosine, col_side[member]).reshape(window, 2, pencil_cols)
        grad_sin = contract_first(sine_table, col_side[member]).reshape(window, 2, pencil_cols)
        grad_re = (grad_cos[:, 0, :] + grad_sin[:, 1, :]) / window
        grad_im = (grad_cos[:, 1, :] - grad_sin[:, 0, :]) / window
        term_re = pupil_re * grad_re + pupil_im * grad_im
        term_im = pupil_re * grad_im - pupil_im * grad_re
        terms.append(
            jnp.stack([term_re, term_im], axis=1)
            .astype(jnp.bfloat16)
            .reshape(window, 2 * pencil_cols)
        )
        win = windows[member].reshape(window, 2, pencil_cols)
        win_re = win[:, 0, :]
        win_im = win[:, 1, :]
        pupil_total = pupil_total + jnp.stack(
            [win_re * grad_re + win_im * grad_im, win_re * grad_im - win_im * grad_re]
        )
    sendback = jnp.take_along_axis(jnp.stack(terms), anchor[:, :, None], axis=1)
    sectioned = sendback.reshape(per_group, groups, col_blocks, strips, 2 * pencil_cols)
    returned = lax.all_to_all(
        lax.all_to_all(sectioned, ("band", "pencil"), split_axis=2, concat_axis=2, tiled=True),
        "led",
        split_axis=1,
        concat_axis=0,
        tiled=True,
    )
    returned = (
        returned.reshape(led_count, col_blocks, strips, 2, pencil_cols)
        .transpose(0, 2, 3, 1, 4)
        .reshape(led_count, strips, 2, window)
    )
    spec_grad = jnp.zeros((local_rows.shape[0], 2, extent), jnp.float32)
    for led_id in range(led_count):
        current = lax.dynamic_slice(
            spec_grad, (first_row[led_id], zero_index, col_start[led_id]), (strips, 2, window)
        )
        current = current + returned[led_id].astype(jnp.float32)
        spec_grad = lax.dynamic_update_slice(
            spec_grad, current, (first_row[led_id], zero_index, col_start[led_id])
        )
    pupil_grad = lax.psum(pupil_total, "led")
    return (spec_grad[None], pupil_grad)


def solution(mesh):
    return jax.shard_map(
        local,
        mesh=mesh,
        in_specs=(
            P(("band", "led", "pencil"), None, None, None),
            P(None, None, ("band", "pencil")),
            P("led", ("band", "pencil"), None),
            P(),
        ),
        out_specs=(
            P(("band", "led", "pencil"), None, None, None),
            P(None, None, ("band", "pencil")),
        ),
        check_vma=False,
    )
```

profile of v0, /device:TPU:0, one launch (start us, length us, event | category | flops | bytes accessed | tf_op | source)
XLA Modules:
  0.0 1357.1 jit_solution(7194177416955352829)
XLA Ops:
  18.4 1.6 fusion.169
  49.6 1.4 convert_element_type.288
  51.0 3.7 copy.148
  54.7 3.9 reshape.1392
  58.6 1.4 copy.91
  60.0 7.4 all-to-all-start
  67.9 17.6 %all-to-all-done = bf16[4,2,16,32,128]{4,2,1,0,3:T(8,128)(2,1)S(1)} async-done(((bf16[4,2,16,32,128]{4,2,1,0,3:T(8,128)(2,1)}), bf16[4,2,16,32,128]{4,2,1,0,3:T(8,128)(2,1)S(1)}, u32[]{:S(2)}, u32[]{:S(2)}) %all-to-all-start) | async-done | bytes 1048608 | tf_op jit(solution)/shard_map/all_to_all | solution.py:61
  86.7 5.5 all-to-all-start.1
  93.3 13.7 %all-to-all-done.1 = bf16[4,2,512,1,128]{4,2,1,3,0:T(8,128)(2,1)S(1)} async-done(((bf16[4,2,512,1,128]{4,2,1,3,0:T(8,128)(2,1)}), bf16[4,2,512,1,128]{4,2,1,3,0:T(8,128)(2,1)S(1)}, u32[]{:S(2)}, u32[]{:S(2)}) %all-to-all-start.1) | async-done | bytes 1048608 | tf_op jit(solution)/shard_map/all_to_all | solution.py:60
  107.1 21.7 %gather_fusion = bf16[4096,128]{1,0:T(8,128)(2,1)S(1)} fusion(bf16[2,2048,128]{2,1,0:T(8,128)(2,1)S(1)} %bitcast.234, s32[4096]{0:T(1024)S(1)} %bitcast.233), kind=kCustom, calls=%fused_computation.clone | custom fusion | bytes 2129920 | tf_op jit(solution)/shard_map/jit(take_along_axis)/gather | solution.py:77
  130.4 62.8 %fusion.24 = f32[128,2048]{1,0:T(8,128)S(1)} fusion(bf16[2048,128]{0,1:T(8,128)(2,1)S(1)} %bitcast.255), kind=kOutput, calls=%fused_computation.31 | convolution fusion | flops 1136656384 | bytes 1572864 | tf_op jit(solution)/shard_map/dot_general | solution.py:17
  193.2 62.5 %fusion.18 = f32[128,2048]{1,0:T(8,128)S(1)} fusion(bf16[2048,128]{0,1:T(8,128)(2,1)S(1)} %bitcast.256), kind=kOutput, calls=%fused_computation.25 | convolution fusion | flops 1136656384 | bytes 1572864 | tf_op jit(solution)/shard_map/dot_general | solution.py:17
  255.8 63.9 %fusion.25 = f32[128,2048]{1,0:T(8,128)} fusion(bf16[2048,128]{0,1:T(8,128)(2,1)S(1)} %bitcast.257), kind=kOutput, calls=%fused_computation.32 | convolution fusion | flops 1136656384 | bytes 1572864 | tf_op jit(solution)/shard_map/dot_general | solution.py:17
  319.7 63.0 %fusion.19 = f32[128,2048]{1,0:T(8,128)} fusion(bf16[2048,128]{0,1:T(8,128)(2,1)S(1)} %bitcast.258), kind=kOutput, calls=%fused_computation.26 | convolution fusion | flops 1136656384 | bytes 1572864 | tf_op jit(solution)/shard_map/dot_general | solution.py:17
  384.4 2.8 pad_maximum_fusion.1
  387.2 1.3 convert_element_type.297
  388.5 1.6 fusion.57
  391.7 3.0 pad_maximum_fusion
  396.7 21.2 %all_to_all.83 = bf16[2,64,32,128]{3,1,0,2:T(8,128)(2,1)S(1)} all-to-all(bf16[2,64,32,128]{3,1,0,2:T(8,128)(2,1)S(1)} %copy.100), channel_id=1, replica_groups=mesh['band'=8,'led'=4,'pencil'=4] {'band','pencil'}, dimensions={2} | all-to-all | bytes 2097152 | tf_op jit(solution)/shard_map/all_to_all | solution.py:105
  418.1 62.9 %fusion.21 = f32[128,2048]{1,0:T(8,128)S(1)} fusion(bf16[2048,128]{1,0:T(8,128)(2,1)S(1)} %bitcast.269), kind=kOutput, calls=%fused_computation.28 | convolution fusion | flops 1136656384 | bytes 1572864 | tf_op jit(solution)/shard_map/dot_general | solution.py:17
  481.0 62.8 %fusion.15 = f32[128,2048]{1,0:T(8,128)S(1)} fusion(bf16[2048,128]{1,0:T(8,128)(2,1)S(1)} %bitcast.270), kind=kOutput, calls=%fused_computation.22 | convolution fusion | flops 1136656384 | bytes 1572864 | tf_op jit(solution)/shard_map/dot_general | solution.py:17
  544.4 63.0 %fusion.20 = f32[128,2048]{1,0:T(8,128)S(1)} fusion(bf16[128,2048]{1,0:T(8,128)(2,1)S(1)} %bitcast.259), kind=kOutput, calls=%fused_computation.27 | convolution fusion | flops 1136656384 | bytes 1572864 | tf_op jit(solution)/shard_map/dot_general | solution.py:124
  607.3 62.5 %fusion.14 = f32[128,2048]{1,0:T(8,128)S(1)} fusion(bf16[128,2048]{1,0:T(8,128)(2,1)S(1)} %bitcast.260), kind=kOutput, calls=%fused_computation.21 | convolution fusion | flops 1136656384 | bytes 1572864 | tf_op jit(solution)/shard_map/dot_general | solution.py:121
  669.8 63.2 %fusion.23 = f32[128,2048]{1,0:T(8,128)S(1)} fusion(bf16[2048,128]{1,0:T(8,128)(2,1)S(1)} %bitcast.267), kind=kOutput, calls=%fused_computation.30 | convolution fusion | flops 1136656384 | bytes 1572864 | tf_op jit(solution)/shard_map/dot_general | solution.py:17
  733.0 62.8 %fusion.17 = f32[128,2048]{1,0:T(8,128)S(1)} fusion(bf16[2048,128]{1,0:T(8,128)(2,1)S(1)} %bitcast.268), kind=kOutput, calls=%fused_computation.24 | convolution fusion | flops 1136656384 | bytes 1572864 | tf_op jit(solution)/shard_map/dot_general | solution.py:17
  796.3 63.6 %fusion.22 = f32[128,2048]{1,0:T(8,128)} fusion(bf16[128,2048]{1,0:T(8,128)(2,1)S(1)} %bitcast.261), kind=kOutput, calls=%fused_computation.29 | convolution fusion | flops 1136656384 | bytes 1572864 | tf_op jit(solution)/shard_map/dot_general | solution.py:124
  860.0 63.1 %fusion.16 = f32[128,2048]{1,0:T(8,128)} fusion(bf16[128,2048]{1,0:T(8,128)(2,1)S(1)} %bitcast.262), kind=kOutput, calls=%fused_computation.23 | convolution fusion | flops 1136656384 | bytes 1572864 | tf_op jit(solution)/shard_map/dot_general | solution.py:121
  924.7 2.8 pad_maximum_fusion.4
  927.5 1.3 convert_element_type.301
  928.8 1.6 fusion.51
  932.0 3.2 pad_maximum_fusion.3
  936.8 1.4 copy.106
  938.2 3.9 all-to-all-start.3
  942.2 18.0 %all-to-all-done.3 = bf16[2,64,32,128]{3,1,0,2:T(8,128)(2,1)S(1)} async-done(((bf16[2,64,32,128]{3,1,0,2:T(8,128)(2,1)}), bf16[2,64,32,128]{3,1,0,2:T(8,128)(2,1)S(1)}, u32[]{:S(2)}, u32[]{:S(2)}) %all-to-all-start.3) | async-done | bytes 1048608 | tf_op jit(solution)/shard_map/all_to_all | solution.py:135
  961.4 62.9 %fusion.6 = f32[2048,2,64]{0,2,1:T(8,128)S(1)} fusion(bf16[2,64,2048]{2,1,0:T(8,128)(2,1)S(1)} %bitcast.263), kind=kOutput, calls=%fused_computation.13 | convolution fusion | flops 1136656384 | bytes 1572864 | tf_op jit(solution)/shard_map/dot_general | solution.py:17
  1024.3 63.7 %fusion.10 = f32[2048,2,64]{0,2,1:T(8,128)S(1)} fusion(bf16[2,64,2048]{2,1,0:T(8,128)(2,1)} %bitcast.264), kind=kOutput, calls=%fused_computation.17 | convolution fusion | flops 1136656384 | bytes 1572864 | tf_op jit(solution)/shard_map/dot_general | solution.py:17
  1088.3 63.2 %fusion.8 = f32[2048,2,64]{0,2,1:T(8,128)S(1)} fusion(bf16[2,64,2048]{2,1,0:T(8,128)(2,1)S(1)} %bitcast.265), kind=kOutput, calls=%fused_computation.15 | convolution fusion | flops 1136656384 | bytes 1572864 | tf_op jit(solution)/shard_map/dot_general | solution.py:17
  1151.4 62.9 %fusion.12 = f32[2048,2,64]{0,2,1:T(8,128)S(1)} fusion(bf16[2,64,2048]{2,1,0:T(8,128)(2,1)S(1)} %bitcast.266), kind=kOutput, calls=%fused_computation.19 | convolution fusion | flops 1136656384 | bytes 1572864 | tf_op jit(solution)/shard_map/dot_general | solution.py:17
  1216.4 1.2 fusion.69
  1221.1 21.7 %gather_fusion.1 = bf16[4096,128]{1,0:T(8,128)(2,1)S(1)} fusion(bf16[2,2048,128]{2,1,0:T(8,128)(2,1)S(1)} %pad_maximum_fusion.6, s32[4096]{0:T(1024)S(1)} %bitcast.232), kind=kCustom, calls=%fused_computation.1.clone | custom fusion | bytes 2129920 | tf_op jit(solution)/shard_map/jit(take_along_axis)/gather | solution.py:158
  1242.9 1.2 broadcast_select_fusion
  1244.4 21.1 %all_to_all.84 = bf16[2,4,32,16,128]{4,3,1,0,2:T(8,128)(2,1)S(1)} all-to-all(bf16[2,4,32,16,128]{4,3,1,0,2:T(8,128)(2,1)S(1)} %copy.112), channel_id=1, replica_groups=mesh['band'=8,'led'=4,'pencil'=4] {'band','pencil'}, dimensions={2} | all-to-all | bytes 2097152 | tf_op jit(solution)/shard_map/all_to_all | solution.py:161
  1266.7 3.5 all-to-all-start.5
  1271.4 17.9 %all-to-all-done.5 = bf16[2,4,32,16,128]{4,3,2,0,1:T(8,128)(2,1)S(1)} async-done(((bf16[2,4,32,16,128]{4,3,2,0,1:T(8,128)(2,1)}), bf16[2,4,32,16,128]{4,3,2,0,1:T(8,128)(2,1)S(1)}, u32[]{:S(2)}, u32[]{:S(2)}) %all-to-all-start.5) | async-done | bytes 1048608 | tf_op jit(solution)/shard_map/all_to_all | solution.py:160
  1290.3 1.4 copy.147
  1291.6 1.5 slice_convert_fusion
  1293.2 1.3 reshape.1431
  1294.5 2.0 reshape.1430
  1298.5 2.4 broadcast_in_dim.20
  1300.9 3.8 dynamic_update_slice.25
  1304.7 1.2 copy_add_fusion.6
  1305.9 4.0 dynamic_update_slice.26
  1309.9 1.2 copy_add_fusion.5
  1311.1 4.0 dynamic_update_slice.27
  1316.3 2.8 dynamic_update_slice.28
  1319.1 1.2 copy_add_fusion.3
  1320.3 4.0 dynamic_update_slice.29
  1324.3 1.2 copy_add_fusion.2
  1326.1 3.9 dynamic_update_slice.30
  1330.0 1.2 copy_add_fusion.1
  1331.2 3.7 dynamic_update_slice.31
  1336.1 4.2 dynamic_update_slice.32
  1340.3 7.4 copy.123
  1347.8 2.3 copy.167
  (107 shorter events, 41.7 us)
Async XLA Ops:
  54.7 12.7 slice-start
  60.0 25.5 %all-to-all-start = ((bf16[4,2,16,32,128]{4,2,1,0,3:T(8,128)(2,1)}), bf16[4,2,16,32,128]{4,2,1,0,3:T(8,128)(2,1)S(1)}, u32[]{:S(2)}, u32[]{:S(2)}) async-start(bf16[4,2,16,32,128]{4,2,1,0,3:T(8,128)(2,1)} %copy.91), calls=%async_computation | async-start | bytes 2097152 | tf_op jit(solution)/shard_map/all_to_all | solution.py:61
  86.7 20.3 %all-to-all-start.1 = ((bf16[4,2,512,1,128]{4,2,1,3,0:T(8,128)(2,1)}), bf16[4,2,512,1,128]{4,2,1,3,0:T(8,128)(2,1)S(1)}, u32[]{:S(2)}, u32[]{:S(2)}) async-start(bf16[4,2,512,1,128]{4,2,1,3,0:T(8,128)(2,1)} %bitcast.26), calls=%async_computation.1 | async-start | bytes 2097152 | tf_op jit(solution)/shard_map/all_to_all | solution.py:60
  128.8 1.2 copy-start.4
  129.6 63.6 %copy-start = (bf16[1,2048,128]{1,2,0:T(8,128)(2,1)}, bf16[1,2048,128]{1,2,0:T(8,128)(2,1)S(1)}, u32[]{:S(2)}) copy-start(bf16[1,2048,128]{1,2,0:T(8,128)(2,1)S(1)} %get-tuple-element.55) | copy-start | bytes 1572868
  129.6 63.6 %copy-start.2 = (bf16[1,2048,128]{1,2,0:T(8,128)(2,1)}, bf16[1,2048,128]{1,2,0:T(8,128)(2,1)S(1)}, u32[]{:S(2)}) copy-start(bf16[1,2048,128]{1,2,0:T(8,128)(2,1)S(1)} %get-tuple-element.56) | copy-start | bytes 1572868
  481.0 62.8 %copy-start.10 = (f32[2,64,2048]{2,1,0:T(8,128)S(1)}, f32[2,64,2048]{2,1,0:T(8,128)}, u32[]{:S(2)}) copy-start(f32[2,64,2048]{2,1,0:T(8,128)} %param.8) | copy-start | bytes 3145732
  935.2 7.0 copy-start.12
  938.2 22.0 %all-to-all-start.3 = ((bf16[2,64,32,128]{3,1,0,2:T(8,128)(2,1)}), bf16[2,64,32,128]{3,1,0,2:T(8,128)(2,1)S(1)}, u32[]{:S(2)}, u32[]{:S(2)}) async-start(bf16[2,64,32,128]{3,1,0,2:T(8,128)(2,1)} %copy.106), calls=%async_computation.3 | async-start | bytes 2097152 | tf_op jit(solution)/shard_map/all_to_all | solution.py:135
  960.6 0.8 copy-start.11
  1151.4 62.9 %copy-start.3 = (bf16[1,2048,128]{1,2,0:T(8,128)(2,1)S(1)}, bf16[1,2048,128]{1,2,0:T(8,128)(2,1)}, u32[]{:S(2)}) copy-start(bf16[1,2048,128]{1,2,0:T(8,128)(2,1)} %copy-done.2) | copy-start | bytes 1572868
  1214.4 1.1 copy-start.1
  1214.4 2.1 copy-start.5
  1221.1 21.7 %copy-start.13 = (pred[2,2048]{1,0:T(4,128)(4,1)S(1)}, pred[2,2048]{1,0:T(4,128)(4,1)}, u32[]{:S(2)}) copy-start(pred[2,2048]{1,0:T(4,128)(4,1)} %get-tuple-element.15) | copy-start | bytes 12292
  1244.1 26.2 %copy-start.6 = (f32[1,2048,64]{1,2,0:T(8,128)S(1)}, f32[1,2048,64]{1,2,0:T(8,128)}, u32[]{:S(2)}) copy-start(f32[1,2048,64]{1,2,0:T(8,128)} %get-tuple-element.9) | copy-start | bytes 1572868
  1244.1 26.2 %copy-start.7 = (f32[1,2048,64]{1,2,0:T(8,128)S(1)}, f32[1,2048,64]{1,2,0:T(8,128)}, u32[]{:S(2)}) copy-start(f32[1,2048,64]{1,2,0:T(8,128)} %get-tuple-element.12) | copy-start | bytes 1572868
  1266.7 22.6 %all-to-all-start.5 = ((bf16[2,4,32,16,128]{4,3,2,0,1:T(8,128)(2,1)}), bf16[2,4,32,16,128]{4,3,2,0,1:T(8,128)(2,1)S(1)}, u32[]{:S(2)}, u32[]{:S(2)}) async-start(bf16[2,4,32,16,128]{4,3,2,0,1:T(8,128)(2,1)} %copy.113), calls=%async_computation.5 | async-start | bytes 2097152 | tf_op jit(solution)/shard_map/all_to_all | solution.py:160
  1270.2 77.6 %all-reduce.2.cloned.1.call-start = ((), (), s32[]{:S(2)}) async-start(), calls=%async_computation.6 | async-start | bytes 2097152 | tf_op jit(solution)/shard_map/psum | solution.py:181
  1298.0 17.2 %copy-start.9 = (f32[16,2,2048]{2,1,0:T(2,128)S(1)}, f32[16,2,2048]{2,1,0:T(2,128)}, u32[]{:S(2)}) copy-start(f32[16,2,2048]{2,1,0:T(2,128)} %reshape.1429) | copy-start | bytes 786436
  1298.5 20.6 %copy-start.8 = (f32[16,2,2048]{2,1,0:T(2,128)S(1)}, f32[16,2,2048]{2,1,0:T(2,128)}, u32[]{:S(2)}) copy-start(f32[16,2,2048]{2,1,0:T(2,128)} %reshape.1430) | copy-start | bytes 786436
Sparse Core Ops, SparseCore 0:
  1273.4 43.7 all-reduce.1
where the time goes:
time: 1370 us; the launch traced here: 1360 us
  matrix products  1010 us (74%)
  local copies, waits for them, and re-layouts  134 us (10%)
  waiting for transfers between devices  67.3 us (5%)
  between operations  45 us (3%)
  blocking collectives  42.3 us (3%)
  other arithmetic  39 us (3%)
  starting transfers between devices  20.4 us (1%)
    dot_general x12, matrix products, contract_first(): lax.dot_general(left, right, (((0,), (0,)), ((), ())), preferred_element_...  757 us
    dot_general x2, matrix products, local(): jnp.dot(residual, sine_table, preferred_element_type=jnp.float32)  127 us
    dot_general x2, matrix products, local(): jnp.dot(residual, cosine, preferred_element_type=jnp.float32)  126 us
    dynamic_update_slice x8, local copies, waits for them, and re-layouts, local(): lax.dynamic_update_slice(spec_grad, current, (first_row[led_id], zero_ind...  30.6 us
  transfers between devices with their start and end apart: 5, of which 4 were waited for; matrix products, arithmetic and copies ran while one was open for 4% of the time, Pallas kernels for 0%

commit v1 on v0

v1 whole, which is shorter than its diff:
```python
import functools
import math

import jax
import jax.numpy as jnp
import ml_dtypes
import numpy as np
from jax import lax
from jax.experimental import pallas as pl
from jax.experimental.pallas import tpu as pltpu
from jax.sharding import PartitionSpec as P

W = 2048
Q = W // 4
LANES = 128
STRIPS = 16
DEVICES = 128
BLOCKS = 32
GROUPS = 4
PER = 2
LEDS = 8
MESH = pl.DeviceIdType.MESH
F32 = jnp.float32
BF16 = jnp.bfloat16


def trig(left, right):
    phase = (np.outer(left, right) % W).astype(np.float64) * (2.0 * math.pi / W)
    return np.cos(phase).astype(np.float32), np.sin(phase).astype(np.float32)


@functools.lru_cache(maxsize=None)
def tables():
    low = np.arange(Q)
    rows_fwd, cols_fwd, cols_back, rows_back = [], [], [], []
    for part in range(4):
        j = (4 * np.arange(32)[:, None] + part + LANES * np.arange(STRIPS)[None, :]).reshape(-1)
        c, s = trig(low, j)
        rows_fwd.append(np.concatenate([c, s], axis=1))
        rows_back.append(np.concatenate([c.T, s.T], axis=1) / W)
        n = 4 * low + part
        c, s = trig(low, n)
        c, s = c.reshape(8, 64, Q), s.reshape(8, 64, Q)
        re = np.concatenate([c, s], axis=2)
        im = np.concatenate([-s, c], axis=2)
        both = np.stack([re, im], axis=1).reshape(2 * Q, 2 * Q)
        cols_fwd.append(both / W)
        cols_back.append(both.T)
    return tuple(np.stack(t).astype(ml_dtypes.bfloat16) for t in (rows_fwd, cols_fwd, cols_back, rows_back))


def lane_id(rows):
    return lax.broadcasted_iota(jnp.int32, (rows, LANES), 1)


def swap(x):
    return pltpu.roll(x, 64, 1)


def position():
    return lax.axis_index("band"), lax.axis_index("led"), lax.axis_index("pencil")


def cut_kernel(off, x, out):
    band, led, pencil = position()
    me = band * 16 + led * 4 + pencil
    lane = lane_id(STRIPS)
    half = lane < 64

    def one(l, carry):
        first = (off[l, 0] - me + (DEVICES - 1)) >> 7
        col = off[l, 1]
        tile, within = col >> 7, col & 127
        keep = lane < LANES - within
        turn = (LANES - within) & 127

        def load(k, part):
            at = first * LANES + 2 * jnp.minimum(tile + k, 63) + part
            return pltpu.roll(x[pl.ds(at, STRIPS, stride=LANES), :], turn, 1)

        re, im = load(0, 0), load(0, 1)
        for k in range(16):
            next_re, next_im = load(k + 1, 0), load(k + 1, 1)
            a = jnp.where(keep, re, next_re)
            b = jnp.where(keep, im, next_im)
            slot = (l >> 1) * BLOCKS + 2 * k
            out[slot, l & 1] = jnp.where(half, a, swap(b)).astype(BF16)
            out[slot + 1, l & 1] = jnp.where(half, swap(a), b).astype(BF16)
            re, im = next_re, next_im
        return carry

    lax.fori_loop(0, LEDS, one, 0)


def add_kernel(off, terms, out):
    band, led, pencil = position()
    me = band * 16 + led * 4 + pencil
    lane = lane_id(STRIPS)
    half = lane < 64

    def clear(i, carry):
        out[pl.ds(pl.multiple_of(i * 256, 256), 256), :] = jnp.zeros((256, LANES), F32)
        return carry

    lax.fori_loop(0, out.shape[0] // 256, clear, 0)

    def one(l, carry):
        first = (off[l, 0] - me + (DEVICES - 1)) >> 7
        col = off[l, 1]
        tile, within = col >> 7, col & 127
        low = lane < within

        def place(k, part):
            return pl.ds(first * LANES + 2 * jnp.minimum(tile + k, 63) + part, STRIPS, stride=LANES)

        zero = jnp.zeros((STRIPS, LANES), F32)
        last = (zero, zero)
        values = []
        for k in range(16):
            slot = (l >> 1) * BLOCKS + 2 * k
            a = terms[slot, l & 1].astype(F32)
            b = terms[slot + 1, l & 1].astype(F32)
            now = (
                pltpu.roll(jnp.where(half, a, swap(b)), within, 1),
                pltpu.roll(jnp.where(half, swap(a), b), within, 1),
            )
            values.append([out[place(k, p), :] + jnp.where(low, last[p], now[p]) for p in range(2)])
            last = now
        for k in range(16):
            for p in range(2):
                out[place(k, p), :] = values[k][p]
        for p in range(2):
            out[place(16, p), :] = out[place(16, p), :] + jnp.where(low, last[p], zero)
        return carry

    lax.fori_loop(0, LEDS, one, 0)


def core_kernel(
    off, send1, pup, meas, h1, h2, h3, h4, recv4, pgout,
    t1, t2, t3, t4, recv1, pup_r, pup_i, tmp_r, tmp_i, perm, smq, x1, ys, send2, recv2, xq, rq, zs,
    send3, recv3, wg, send4, pg, pg16, rsr, agr,
    tsem, s1, r1, s2, r2, s3, r3, s4, r4, s5, r5, s6, r6,
):
    band, led, pencil = position()
    me = band * 16 + led * 4 + pencil
    block = band * 4 + pencil
    slot_me = led * BLOCKS + block
    sgn = jnp.where(lane_id(1) < 64, -1.0, 1.0).astype(F32)

    def device(d):
        return {"band": d >> 4, "led": (d >> 2) & 3, "pencil": d & 3}

    def plane(b):
        return {"band": b >> 2, "led": led, "pencil": b & 3}

    fetch = [pltpu.make_async_copy(h, t, tsem.at[i]) for i, (h, t) in enumerate(((h1, t1), (h2, t2), (h3, t3), (h4, t4)))]
    for f in fetch:
        f.start()

    barrier = pltpu.get_barrier_semaphore()

    def greet(i, c):
        pl.semaphore_signal(barrier, inc=1, device_id=device((me + i) & 127), device_id_type=MESH)
        return c

    lax.fori_loop(1, DEVICES, greet, 0)
    pl.semaphore_wait(barrier, DEVICES - 1)

    def start1(i, c):
        d = (me + i) & 127
        slot = ((d >> 2) & 3) * BLOCKS + (d >> 4) * 4 + (d & 3)
        pltpu.make_async_remote_copy(
            src_ref=send1.at[slot], dst_ref=recv1.at[me], send_sem=s1, recv_sem=r1, device_id=device(d), device_id_type=MESH
        ).start()
        return c

    pltpu.make_async_copy(send1.at[slot_me], recv1.at[me], r1).start()
    lax.fori_loop(1, DEVICES, start1, 0)

    def turn(s, c):
        blk = pup[:, pl.ds(pl.multiple_of(s * LANES, LANES), LANES)].T
        other = swap(blk)
        half = lane_id(LANES) < 64
        tmp_r[...] = jnp.where(half, blk, other)
        tmp_i[...] = jnp.where(half, other, blk) * sgn
        for v in range(4):
            pup_r[v * 32 : (v + 1) * 32, s, :] = tmp_r[pl.ds(v, 32, stride=4), :]
            pup_i[v * 32 : (v + 1) * 32, s, :] = tmp_i[pl.ds(v, 32, stride=4), :]
        return c

    lax.fori_loop(0, STRIPS, turn, 0)

    src = lax.broadcasted_iota(jnp.int32, (Q, Q), 0)
    dst = lax.broadcasted_iota(jnp.int32, (Q, Q), 1)
    perm[...] = jnp.where(src == 4 * (dst & 127) + (dst >> 7), 1.0, 0.0).astype(BF16)
    for g in range(4):
        root = jnp.sqrt(meas[:, g * Q : (g + 1) * Q])
        high = root.astype(BF16)
        low = (root - high.astype(F32)).astype(BF16)
        moved = jnp.dot(high, perm[...], preferred_element_type=F32) + jnp.dot(low, perm[...], preferred_element_type=F32)
        for q in range(4):
            smq[q, :, g * LANES : (g + 1) * LANES] = moved[:, q * LANES : (q + 1) * LANES]

    fetch[0].wait()
    pltpu.make_async_copy(recv1, recv1, r1).wait()

    def shift(e):
        return off[led * PER + e, 0] & 127

    def send_plane(src, dst, ssem, rsem):
        pltpu.make_async_copy(src.at[pl.ds(pl.multiple_of(block * 64, 64), 64)], dst.at[block], rsem).start()

        def go(i, c):
            b = (block + i) & 31
            pltpu.make_async_remote_copy(
                src_ref=src.at[pl.ds(pl.multiple_of(b * 64, 64), 64)],
                dst_ref=dst.at[block],
                send_sem=ssem,
                recv_sem=rsem,
                device_id=plane(b),
                device_id_type=MESH,
            ).start()
            return c

        lax.fori_loop(1, BLOCKS, go, 0)

    for e in range(PER):
        delta = shift(e)

        def product(w, c):
            d = 4 * (w & 31) + (w >> 5)
            win = recv1[(d + delta) & 127, e].astype(F32)
            prod = win * pup_r[w] + swap(win) * pup_i[w]
            at = pl.multiple_of((w & 31) * STRIPS, STRIPS)
            x1[w >> 5, pl.ds(at, STRIPS), :] = prod.astype(BF16)
            x1[w >> 5, pl.ds(at + Q, STRIPS), :] = (swap(prod) * sgn).astype(BF16)
            return c

        lax.fori_loop(0, DEVICES, product, 0, unroll=8)

        def first(v, c):
            ys[v] = jnp.dot(t1[v], x1[v], preferred_element_type=F32)
            return c

        lax.fori_loop(0, 4, first, 0)

        def butterfly(i, c):
            at = pl.multiple_of(i * 64, 64)
            rows = pl.ds(at, 64)
            y0, y1, y2, y3 = (ys[v, rows, :] for v in range(4))
            even, odd = y0 + y2, y1 + y3
            diff, turned = y0 - y2, swap(y1 - y3) * sgn
            for u, value in enumerate((even + odd, diff + turned, even - odd, diff - turned)):
                send2[e, pl.ds(at + u * Q, 64), :] = value.astype(BF16)
            return c

        lax.fori_loop(0, 8, butterfly, 0)
        send_plane(send2.at[e], recv2.at[e], s2.at[e], r2.at[e])

    fetch[1].wait()
    fetch[2].wait()
    for e in range(PER):
        pltpu.make_async_copy(recv2.at[e], recv2.at[e], r2.at[e]).wait()
        for b in range(8):
            a0, a1, a2, a3 = (recv2[e, b + 8 * u].astype(F32) for u in range(4))
            even, odd = a0 + a2, a1 + a3
            diff, turned = a0 - a2, swap(a1 - a3) * sgn
            for q, value in enumerate((even + odd, diff + turned, even - odd, diff - turned)):
                xq[q, :, b * LANES : (b + 1) * LANES] = value.astype(BF16)

        def field(q, c):
            got = jnp.dot(xq[q], t2[q], preferred_element_type=F32)
            re, im = got[:, :Q], got[:, Q:]
            factor = 1.0 - smq[q, pl.ds(e * 64, 64), :] * lax.rsqrt(jnp.maximum(re * re + im * im, 0.25))
            rq[:, :Q] = (re * factor).astype(BF16)
            rq[:, Q:] = (im * factor).astype(BF16)
            zs[q] = jnp.dot(rq[...], t3[q], preferred_element_type=F32)
            return c

        lax.fori_loop(0, 4, field, 0)
        for b in range(8):
            z0, z1, z2, z3 = (zs[q, :, b * LANES : (b + 1) * LANES] for q in range(4))
            even, odd = z0 + z2, z1 + z3
            diff, turned = z0 - z2, swap(z1 - z3) * sgn
            for u, value in enumerate((even + odd, diff - turned, even - odd, diff + turned)):
                send3[e, (b + 8 * u) * 64 : (b + 8 * u + 1) * 64, :] = value.astype(BF16)
        send_plane(send3.at[e], recv3.at[e], s3.at[e], r3.at[e])

    fetch[3].wait()
    for e in range(PER):
        pltpu.make_async_copy(recv3.at[e], recv3.at[e], r3.at[e]).wait()
        delta = shift(e)

        def fold(i, c):
            at = pl.multiple_of(i * 64, 64)
            a0, a1, a2, a3 = (recv3[e, i + 8 * u].astype(F32) for u in range(4))
            even, odd = a0 + a2, a1 + a3
            diff, turned = a0 - a2, swap(a1 - a3) * sgn
            for q, value in enumerate((even + odd, diff - turned, even - odd, diff + turned)):
                x1[q, pl.ds(at, 64), :] = value.astype(BF16)
                x1[q, pl.ds(at + Q, 64), :] = (swap(value) * (-sgn)).astype(BF16)
            return c

        lax.fori_loop(0, 8, fold, 0)

        def last(q, c):
            got = jnp.dot(t4[q], x1[q], preferred_element_type=F32)
            wg[e, pl.ds(q * 32, 32)] = got.reshape(32, STRIPS, LANES)
            return c

        lax.fori_loop(0, 4, last, 0)

        def pupil_sum(w, c):
            rows = pl.ds(pl.multiple_of(w * STRIPS, STRIPS), STRIPS)
            d = 4 * (w & 31) + (w >> 5)
            win = recv1[(d + delta) & 127, e].astype(F32)
            grad = wg[e, w]
            other = swap(win)
            half = lane_id(STRIPS) < 64
            value = grad * jnp.where(half, win, other) - swap(grad) * (jnp.where(half, other, win) * sgn)
            if e == 0:
                pg[rows, :] = value
            else:
                value = value + pg[rows, :]
                pg[rows, :] = value
                pg16[w >> 5, pl.ds(pl.multiple_of((w & 31) * STRIPS, STRIPS), STRIPS), :] = value.astype(BF16)
            return c

        lax.fori_loop(0, DEVICES, pupil_sum, 0, unroll=8)

        def term(d, c):
            w0 = (d - delta) & 127
            w = (w0 & 3) * 32 + (w0 >> 2)
            grad = wg[e, w]
            send4[d, e] = (grad * pup_r[w] - swap(grad) * pup_i[w]).astype(BF16)
            return c

        lax.fori_loop(0, DEVICES, term, 0, unroll=8)

    def along(i):
        return {"band": band, "led": (led + i) & 3, "pencil": pencil}

    for i in range(1, GROUPS):
        pltpu.make_async_remote_copy(
            src_ref=pg16.at[(led + i) & 3], dst_ref=rsr.at[led], send_sem=s5.at[i - 1], recv_sem=r5,
            device_id=along(i), device_id_type=MESH,
        ).start()

    def start4(i, c):
        d = (me + i) & 127
        pltpu.make_async_remote_copy(
            src_ref=send4.at[d], dst_ref=recv4.at[slot_me], send_sem=s4, recv_sem=r4, device_id=device(d), device_id_type=MESH
        ).start()
        return c

    pltpu.make_async_copy(send4.at[me], recv4.at[slot_me], r4).start()
    lax.fori_loop(1, DEVICES, start4, 0)

    pltpu.make_async_copy(rsr.at[pl.ds(0, 3)], rsr.at[pl.ds(0, 3)], r5).wait()
    total = pg[pl.ds(pl.multiple_of(led * Q, Q), Q), :]
    for i in range(1, GROUPS):
        total = total + rsr[(led + i) & 3].astype(F32)
    agr[led] = total.astype(BF16)
    for i in range(1, GROUPS):
        pltpu.make_async_remote_copy(
            src_ref=agr.at[led], dst_ref=agr.at[led], send_sem=s6.at[i - 1], recv_sem=r6,
            device_id=along(i), device_id_type=MESH,
        ).start()
    pltpu.make_async_copy(agr.at[pl.ds(0, 3)], agr.at[pl.ds(0, 3)], r6).wait()

    for v in range(4):
        pg[v * Q : (v + 1) * Q, :] = agr[v].astype(F32)

    def back(s, c):
        for v in range(4):
            tmp_r[pl.ds(v, 32, stride=4), :] = pg[pl.ds(v * Q + s, 32, stride=STRIPS), :]
        pgout[:, pl.ds(pl.multiple_of(s * LANES, LANES), LANES)] = tmp_r[...].T
        return c

    lax.fori_loop(0, STRIPS, back, 0)

    pltpu.make_async_copy(send1.at[pl.ds(0, 127)], send1.at[pl.ds(0, 127)], s1).wait()
    for e in range(PER):
        part = pl.ds(0, W - 64)
        pltpu.make_async_copy(send2.at[e, part], send2.at[e, part], s2.at[e]).wait()
        pltpu.make_async_copy(send3.at[e, part], send3.at[e, part], s3.at[e]).wait()
    for i in range(1, GROUPS):
        pltpu.make_async_copy(pg16.at[0], pg16.at[0], s5.at[i - 1]).wait()
        pltpu.make_async_copy(agr.at[0], agr.at[0], s6.at[i - 1]).wait()
    pltpu.make_async_copy(send4.at[pl.ds(0, 127)], send4.at[pl.ds(0, 127)], s4).wait()
    pltpu.make_async_copy(recv4, recv4, r4).wait()


VMEM = pl.BlockSpec(memory_space=pltpu.VMEM)
SMEM = pl.BlockSpec(memory_space=pltpu.SMEM)
ANY = pl.BlockSpec(memory_space=pl.ANY)
EXCHANGE = (DEVICES, PER, STRIPS, LANES)


def local(spectrum, pupil, measured, offsets):
    small = pltpu.CompilerParams(vmem_limit_bytes=24 << 20)
    rows = spectrum.shape[1]
    tiles = spectrum.shape[3] // LANES
    x = spectrum.reshape(rows, 2, tiles, LANES).transpose(0, 2, 1, 3).reshape(rows * tiles * 2, LANES)
    send1 = pl.pallas_call(
        cut_kernel, out_shape=jax.ShapeDtypeStruct(EXCHANGE, BF16), in_specs=[SMEM, VMEM], out_specs=VMEM,
        compiler_params=small, name="cut",
    )(offsets, x)
    pup = pupil.transpose(0, 2, 1).reshape(LANES, W)
    meas = measured.reshape(PER * 64, W)
    dma = pltpu.SemaphoreType.DMA
    recv4, pgrad = pl.pallas_call(
        core_kernel,
        out_shape=(jax.ShapeDtypeStruct(EXCHANGE, BF16), jax.ShapeDtypeStruct((LANES, W), F32)),
        in_specs=[SMEM, VMEM, VMEM, VMEM, ANY, ANY, ANY, ANY],
        out_specs=(VMEM, VMEM),
        scratch_shapes=[
            pltpu.VMEM((4, Q, 2 * Q), BF16),
            pltpu.VMEM((4, 2 * Q, 2 * Q), BF16),
            pltpu.VMEM((4, 2 * Q, 2 * Q), BF16),
            pltpu.VMEM((4, Q, 2 * Q), BF16),
            pltpu.VMEM(EXCHANGE, BF16),
            pltpu.VMEM((DEVICES, STRIPS, LANES), F32),
            pltpu.VMEM((DEVICES, STRIPS, LANES), F32),
            pltpu.VMEM((LANES, LANES), F32),
            pltpu.VMEM((LANES, LANES), F32),
            pltpu.VMEM((Q, Q), BF16),
            pltpu.VMEM((4, PER * 64, Q), F32),
            pltpu.VMEM((4, 2 * Q, LANES), BF16),
            pltpu.VMEM((4, Q, LANES), F32),
            pltpu.VMEM((PER, W, LANES), BF16),
            pltpu.VMEM((PER, BLOCKS, 64, LANES), BF16),
            pltpu.VMEM((4, 64, 2 * Q), BF16),
            pltpu.VMEM((64, 2 * Q), BF16),
            pltpu.VMEM((4, 64, 2 * Q), F32),
            pltpu.VMEM((PER, W, LANES), BF16),
            pltpu.VMEM((PER, BLOCKS, 64, LANES), BF16),
            pltpu.VMEM((PER, DEVICES, STRIPS, LANES), F32),
            pltpu.VMEM(EXCHANGE, BF16),
            pltpu.VMEM((W, LANES), F32),
            pltpu.VMEM((4, Q, LANES), BF16),
            pltpu.VMEM((4, Q, LANES), BF16),
            pltpu.VMEM((4, Q, LANES), BF16),
            dma((4,)), dma, dma, dma((PER,)), dma((PER,)), dma((PER,)), dma((PER,)),
            dma, dma, dma((3,)), dma, dma((3,)), dma,
        ],
        compiler_params=pltpu.CompilerParams(collective_id=0, has_side_effects=True, vmem_limit_bytes=58 << 20),
        name="core",
    )(offsets, send1, pup, meas, *(jnp.asarray(t) for t in tables()))
    total = pl.pallas_call(
        add_kernel, out_shape=jax.ShapeDtypeStruct(x.shape, F32), in_specs=[SMEM, VMEM], out_specs=VMEM,
        compiler_params=small, name="add",
    )(offsets, recv4)
    spec_grad = total.reshape(rows, tiles, 2, LANES).transpose(0, 2, 1, 3).reshape(spectrum.shape)
    return spec_grad, pgrad.reshape(2, 64, W).transpose(0, 2, 1)


def solution(mesh):
    return jax.shard_map(
        local,
        mesh=mesh,
        in_specs=(
            P(("band", "led", "pencil"), None, None, None),
            P(None, None, ("band", "pencil")),
            P("led", ("band", "pencil"), None),
            P(),
        ),
        out_specs=(
            P(("band", "led", "pencil"), None, None, None),
            P(None, None, ("band", "pencil")),
        ),
        check_vma=False,
    )
```

time: 1370 us -> 120 us (0.09)
  matrix products: 1010 us -> 0 us
  local copies, waits for them, and re-layouts: 134 us -> 6.79 us
  Pallas kernels: 0 us -> 112 us
  waiting for transfers between devices: 67.3 us -> 0 us
  between operations: 45 us -> 0.66 us
  blocking collectives: 42.3 us -> 0 us
  other arithmetic: 39 us -> 0 us
  starting transfers between devices: 20.4 us -> 0 us
    dot_general x16 -> x0, matrix products: 1010 us -> none  [the longest x12 757 us: contract_first(): lax.dot_general(left, right, (((0,), (0,)), ((), ())), preferred_element_...]
    pallas_call x0 -> x3, Pallas kernels: none -> 112 us  [the longest x1 102 us: local(): pl.pallas_call(core_kernel, out_shape=(jax.ShapeDtypeStruct(EXCHANGE, BF1...]
    all_to_all x4 -> x0, waiting for transfers between devices: 67.3 us -> none  [the longest x1 18 us: local(): lax.all_to_all(back_all, ('band', 'pencil'), split_axis=2, concat_axis=1,...]
    gather x3 -> x0, local copies, waits for them, and re-layouts: 43.9 us -> none  [the longest x2 22.2 us: local(): jnp.take_along_axis(received.reshape(per_group, window, 2 * pencil_cols),...]
    all_to_all x2 -> x0, blocking collectives: 42.3 us -> none  [the longest x1 21.2 us: local(): lax.all_to_all(half_all, ('band', 'pencil'), split_axis=2, concat_axis=1,...]
    dynamic_update_slice x8 -> x0, local copies, waits for them, and re-layouts: 30.6 us -> none  [local(): lax.dynamic_update_slice(spec_grad, current, (first_row[led_id], zero_ind...]
    another operation x21 -> x0, other arithmetic: 22.5 us -> none
    all_to_all x4 -> x0, starting transfers between devices: 20.4 us -> none  [the longest x1 7.4 us: local(): lax.all_to_all(outgoing, ('band', 'pencil'), split_axis=3, concat_axis=2,...]
  transfers between devices with their start and end apart: 5 -> 0, of which waited for: 4 -> 0; matrix products, arithmetic and copies ran while one was open for 4% -> 0% of each run, Pallas kernels for 0% -> 0%
where the time goes in v1:
time: 120 us; the launch traced here: 119 us
  Pallas kernels  112 us (93%)
  local copies, waits for them, and re-layouts  6.79 us (6%)
    pallas_call x1, Pallas kernels, local(): pl.pallas_call(core_kernel, out_shape=(jax.ShapeDtypeStruct(EXCHANGE, BF1...  102 us
    pallas_call x1, Pallas kernels, local(): pl.pallas_call(add_kernel, out_shape=jax.ShapeDtypeStruct(x.shape, F32),...  6.85 us
    unnamed x14, local copies, waits for them, and re-layouts  6.79 us
    pallas_call x1, Pallas kernels, local(): pl.pallas_call(cut_kernel, out_shape=jax.ShapeDtypeStruct(EXCHANGE, BF16)...  3.01 us

profile of v1, /device:TPU:0, one launch (start us, length us, event | category | flops | bytes accessed | tf_op | source)
XLA Modules:
  0.0 119.3 jit_solution(16604114641894904310)
XLA Ops:
  0.6 0.8 copy.13.off
  1.4 0.0 copy-start
  1.4 2.2 %copy-done = f32[1,64,2,8192]{3,2,1,0:T(2,128)S(1)} copy-done((f32[1,64,2,8192]{3,2,1,0:T(2,128)S(1)}, f32[1,64,2,8192]{3,2,1,0:T(2,128)}, u32[]{:S(2)}) %copy-start) | copy-done | bytes 4194328
  3.6 0.0 copy-start.3
  3.6 3.0 %cut.1.send1 = bf16[128,2,16,128]{3,2,1,0:T(8,128)(2,1)S(1)} custom-call(s32[8,2]{1,0:T(8,128)S(1)} %copy.13.off, f32[8192,128]{1,0:T(8,128)S(1)} %bitcast.17), custom_call_target="tpu_custom_call" | custom-call | tf_op jit(solution)/shard_map/cut/pallas_call | solution.py:406
  6.6 0.0 copy-done.3
  6.6 0.0 copy-start.1
  6.6 1.0 copy-done.1
  7.6 102.0 %core.1 = (bf16[128,2,16,128]{3,2,1,0:T(8,128)(2,1)}, f32[128,2048]{1,0:T(8,128)}) custom-call(s32[8,2]{1,0:T(8,128)} %copy-done.3, bf16[128,2,16,128]{3,2,1,0:T(8,128)(2,1)} %copy-done.1, f32[128,2048]{1,0:T(8,128)} %bitcast.20, f32[128,2048]{1,0:T(8,128)} %bitcast.21, bf16[4,512,1024]{2,1,0:T(8,128)(2,1)} %constant.8.clone.h1, ...), custom_call_target="tpu_custom_call" | custom-call | tf_op jit(solution)/shard_map/core/pallas_call | solution.py:413
  109.5 0.0 copy-start.2
  109.5 1.2 %copy-done.2 = bf16[128,2,16,128]{3,2,1,0:T(8,128)(2,1)S(1)} copy-done((bf16[128,2,16,128]{3,2,1,0:T(8,128)(2,1)S(1)}, bf16[128,2,16,128]{3,2,1,0:T(8,128)(2,1)}, u32[]{:S(2)}) %copy-start.2) | copy-done | bytes 1048600
  110.8 0.0 copy-start.4
  110.8 0.7 copy-done.4
  111.4 0.0 copy-start.5
  111.4 6.8 %add.1 = f32[8192,128]{1,0:T(8,128)} custom-call(s32[8,2]{1,0:T(8,128)S(1)} %copy-done.4, bf16[128,2,16,128]{3,2,1,0:T(8,128)(2,1)S(1)} %copy-done.2), custom_call_target="tpu_custom_call" | custom-call | tf_op jit(solution)/shard_map/add/pallas_call | solution.py:451
  118.3 0.0 copy-done.5
  118.3 1.0 copy.16
Async XLA Ops:
  1.4 2.2 %copy-start = (f32[1,64,2,8192]{3,2,1,0:T(2,128)S(1)}, f32[1,64,2,8192]{3,2,1,0:T(2,128)}, u32[]{:S(2)}) copy-start(f32[1,64,2,8192]{3,2,1,0:T(2,128)} %param.8) | copy-start | bytes 12582916
  3.6 3.0 %copy-start.3 = (s32[8,2]{1,0:T(8,128)}, s32[8,2]{1,0:T(8,128)S(1)}, u32[]{:S(2)}) copy-start(s32[8,2]{1,0:T(8,128)S(1)} %copy.13.off) | copy-start | bytes 196
  6.6 1.0 copy-start.1
  109.5 1.2 %copy-start.2 = (bf16[128,2,16,128]{3,2,1,0:T(8,128)(2,1)S(1)}, bf16[128,2,16,128]{3,2,1,0:T(8,128)(2,1)}, u32[]{:S(2)}) copy-start(bf16[128,2,16,128]{3,2,1,0:T(8,128)(2,1)} %get-tuple-element.4.terms) | copy-start | bytes 3145732
  110.8 0.7 copy-start.4
  111.4 6.9 %copy-start.5 = (f32[128,2048]{1,0:T(8,128)S(1)}, f32[128,2048]{1,0:T(8,128)}, u32[]{:S(2)}) copy-start(f32[128,2048]{1,0:T(8,128)} %get-tuple-element.5) | copy-start | bytes 3145732

commit v2 on v1

--- a/solution.py
+++ b/solution.py
@@ -19,6 +19,7 @@
 GROUPS = 4
 PER = 2
 LEDS = 8
+STEP = 11
 MESH = pl.DeviceIdType.MESH
 F32 = jnp.float32
 BF16 = jnp.bfloat16
@@ -68,8 +69,8 @@
     half = lane < 64
 
     def one(l, carry):
-        first = (off[l, 0] - me + (DEVICES - 1)) >> 7
-        col = off[l, 1]
+        first = (off[0, l] - me + (DEVICES - 1)) >> 7
+        col = off[1, l]
         tile, within = col >> 7, col & 127
         keep = lane < LANES - within
         turn = (LANES - within) & 127
@@ -84,15 +85,15 @@
             a = jnp.where(keep, re, next_re)
             b = jnp.where(keep, im, next_im)
             slot = (l >> 1) * BLOCKS + 2 * k
-            out[slot, l & 1] = jnp.where(half, a, swap(b)).astype(BF16)
-            out[slot + 1, l & 1] = jnp.where(half, swap(a), b).astype(BF16)
+            out[l & 1, slot] = jnp.where(half, a, swap(b)).astype(BF16)
+            out[l & 1, slot + 1] = jnp.where(half, swap(a), b).astype(BF16)
             re, im = next_re, next_im
         return carry
 
     lax.fori_loop(0, LEDS, one, 0)
 
 
-def add_kernel(off, terms, out):
+def add_kernel(off, terms, pgrad, out, pgrad_out):
     band, led, pencil = position()
     me = band * 16 + led * 4 + pencil
     lane = lane_id(STRIPS)
@@ -103,10 +104,11 @@
         return carry
 
     lax.fori_loop(0, out.shape[0] // 256, clear, 0)
+    pgrad_out[...] = pgrad[...]
 
     def one(l, carry):
-        first = (off[l, 0] - me + (DEVICES - 1)) >> 7
-        col = off[l, 1]
+        first = (off[0, l] - me + (DEVICES - 1)) >> 7
+        col = off[1, l]
         tile, within = col >> 7, col & 127
         low = lane < within
 
@@ -118,8 +120,8 @@
         values = []
         for k in range(16):
             slot = (l >> 1) * BLOCKS + 2 * k
-            a = terms[slot, l & 1].astype(F32)
-            b = terms[slot + 1, l & 1].astype(F32)
+            a = terms[l & 1, slot].astype(F32)
+            b = terms[l & 1, slot + 1].astype(F32)
             now = (
                 pltpu.roll(jnp.where(half, a, swap(b)), within, 1),
                 pltpu.roll(jnp.where(half, swap(a), b), within, 1),
@@ -138,10 +140,11 @@
 
 def core_kernel(
     off, send1, pup, meas, h1, h2, h3, h4, recv4, pgout,
-    t1, t2, t3, t4, recv1, pup_r, pup_i, tmp_r, tmp_i, perm, smq, x1, ys, send2, recv2, xq, rq, zs,
+    t1, t2, t3, t4, recv1_0, recv1_1, pup_r, pup_i, tmp_r, tmp_i, perm, smq, x1, ys, send2, recv2, xq, rq, zs,
     send3, recv3, wg, send4, pg, pg16, rsr, agr,
     tsem, s1, r1, s2, r2, s3, r3, s4, r4, s5, r5, s6, r6,
 ):
+    recv1 = (recv1_0, recv1_1)
     band, led, pencil = position()
     me = band * 16 + led * 4 + pencil
     block = band * 4 + pencil
@@ -167,16 +170,19 @@
     lax.fori_loop(1, DEVICES, greet, 0)
     pl.semaphore_wait(barrier, DEVICES - 1)
 
-    def start1(i, c):
-        d = (me + i) & 127
-        slot = ((d >> 2) & 3) * BLOCKS + (d >> 4) * 4 + (d & 3)
-        pltpu.make_async_remote_copy(
-            src_ref=send1.at[slot], dst_ref=recv1.at[me], send_sem=s1, recv_sem=r1, device_id=device(d), device_id_type=MESH
-        ).start()
-        return c
-
-    pltpu.make_async_copy(send1.at[slot_me], recv1.at[me], r1).start()
-    lax.fori_loop(1, DEVICES, start1, 0)
+    for e in range(PER):
+
+        def start1(i, c):
+            d = (me + i * STEP) & 127
+            slot = ((d >> 2) & 3) * BLOCKS + (d >> 4) * 4 + (d & 3)
+            pltpu.make_async_remote_copy(
+                src_ref=send1.at[e, slot], dst_ref=recv1[e].at[me], send_sem=s1.at[e], recv_sem=r1.at[e],
+                device_id=device(d), device_id_type=MESH,
+            ).start()
+            return c
+
+        pltpu.make_async_copy(send1.at[e, slot_me], recv1[e].at[me], r1.at[e]).start()
+        lax.fori_loop(1, DEVICES, start1, 0)
 
     def turn(s, c):
         blk = pup[:, pl.ds(pl.multiple_of(s * LANES, LANES), LANES)].T
@@ -203,16 +209,15 @@
             smq[q, :, g * LANES : (g + 1) * LANES] = moved[:, q * LANES : (q + 1) * LANES]
 
     fetch[0].wait()
-    pltpu.make_async_copy(recv1, recv1, r1).wait()
 
     def shift(e):
-        return off[led * PER + e, 0] & 127
+        return off[0, led * PER + e] & 127
 
     def send_plane(src, dst, ssem, rsem):
         pltpu.make_async_copy(src.at[pl.ds(pl.multiple_of(block * 64, 64), 64)], dst.at[block], rsem).start()
 
         def go(i, c):
-            b = (block + i) & 31
+            b = (block + i * STEP) & 31
             pltpu.make_async_remote_copy(
                 src_ref=src.at[pl.ds(pl.multiple_of(b * 64, 64), 64)],
                 dst_ref=dst.at[block],
@@ -226,11 +231,12 @@
         lax.fori_loop(1, BLOCKS, go, 0)
 
     for e in range(PER):
+        pltpu.make_async_copy(recv1[e], recv1[e], r1.at[e]).wait()
         delta = shift(e)
 
         def product(w, c):
             d = 4 * (w & 31) + (w >> 5)
-            win = recv1[(d + delta) & 127, e].astype(F32)
+            win = recv1[e][(d + delta) & 127].astype(F32)
             prod = win * pup_r[w] + swap(win) * pup_i[w]
             at = pl.multiple_of((w & 31) * STRIPS, STRIPS)
             x1[w >> 5, pl.ds(at, STRIPS), :] = prod.astype(BF16)
@@ -288,6 +294,9 @@
         send_plane(send3.at[e], recv3.at[e], s3.at[e], r3.at[e])
 
     fetch[3].wait()
+    def along(i):
+        return {"band": band, "led": (led + i) & 3, "pencil": pencil}
+
     for e in range(PER):
         pltpu.make_async_copy(recv3.at[e], recv3.at[e], r3.at[e]).wait()
         delta = shift(e)
@@ -306,7 +315,7 @@
 
         def last(q, c):
             got = jnp.dot(t4[q], x1[q], preferred_element_type=F32)
-            wg[e, pl.ds(q * 32, 32)] = got.reshape(32, STRIPS, LANES)
+            wg[pl.ds(q * 32, 32)] = got.reshape(32, STRIPS, LANES)
             return c
 
         lax.fori_loop(0, 4, last, 0)
@@ -314,8 +323,8 @@
         def pupil_sum(w, c):
             rows = pl.ds(pl.multiple_of(w * STRIPS, STRIPS), STRIPS)
             d = 4 * (w & 31) + (w >> 5)
-            win = recv1[(d + delta) & 127, e].astype(F32)
-            grad = wg[e, w]
+            win = recv1[e][(d + delta) & 127].astype(F32)
+            grad = wg[w]
             other = swap(win)
             half = lane_id(STRIPS) < 64
             value = grad * jnp.where(half, win, other) - swap(grad) * (jnp.where(half, other, win) * sgn)
@@ -327,35 +336,33 @@
                 pg16[w >> 5, pl.ds(pl.multiple_of((w & 31) * STRIPS, STRIPS), STRIPS), :] = value.astype(BF16)
             return c
 
-        lax.fori_loop(0, DEVICES, pupil_sum, 0, unroll=8)
-
         def term(d, c):
             w0 = (d - delta) & 127
             w = (w0 & 3) * 32 + (w0 >> 2)
-            grad = wg[e, w]
-            send4[d, e] = (grad * pup_r[w] - swap(grad) * pup_i[w]).astype(BF16)
-            return c
-
+            grad = wg[w]
+            send4[e, d] = (grad * pup_r[w] - swap(grad) * pup_i[w]).astype(BF16)
+            return c
+
+        def start4(i, c):
+            d = (me + i * STEP) & 127
+            pltpu.make_async_remote_copy(
+                src_ref=send4.at[e, d], dst_ref=recv4.at[e, slot_me], send_sem=s4.at[e], recv_sem=r4.at[e],
+                device_id=device(d), device_id_type=MESH,
+            ).start()
+            return c
+
+        if e > 0:
+            lax.fori_loop(0, DEVICES, pupil_sum, 0, unroll=8)
+            for i in range(1, GROUPS):
+                pltpu.make_async_remote_copy(
+                    src_ref=pg16.at[(led + i) & 3], dst_ref=rsr.at[led], send_sem=s5.at[i - 1], recv_sem=r5,
+                    device_id=along(i), device_id_type=MESH,
+                ).start()
         lax.fori_loop(0, DEVICES, term, 0, unroll=8)
-
-    def along(i):
-        return {"band": band, "led": (led + i) & 3, "pencil": pencil}
-
-    for i in range(1, GROUPS):
-        pltpu.make_async_remote_copy(
-            src_ref=pg16.at[(led + i) & 3], dst_ref=rsr.at[led], send_sem=s5.at[i - 1], recv_sem=r5,
-            device_id=along(i), device_id_type=MESH,
-        ).start()
-
-    def start4(i, c):
-        d = (me + i) & 127
-        pltpu.make_async_remote_copy(
-            src_ref=send4.at[d], dst_ref=recv4.at[slot_me], send_sem=s4, recv_sem=r4, device_id=device(d), device_id_type=MESH
-        ).start()
-        return c
-
-    pltpu.make_async_copy(send4.at[me], recv4.at[slot_me], r4).start()
-    lax.fori_loop(1, DEVICES, start4, 0)
+        pltpu.make_async_copy(send4.at[e, me], recv4.at[e, slot_me], r4.at[e]).start()
+        lax.fori_loop(1, DEVICES, start4, 0)
+        if e == 0:
+            lax.fori_loop(0, DEVICES, pupil_sum, 0, unroll=8)
 
     pltpu.make_async_copy(rsr.at[pl.ds(0, 3)], rsr.at[pl.ds(0, 3)], r5).wait()
     total = pg[pl.ds(pl.multiple_of(led * Q, Q), Q), :]
@@ -380,25 +387,27 @@
 
     lax.fori_loop(0, STRIPS, back, 0)
 
-    pltpu.make_async_copy(send1.at[pl.ds(0, 127)], send1.at[pl.ds(0, 127)], s1).wait()
     for e in range(PER):
+        part = pl.ds(0, DEVICES - 1)
+        pltpu.make_async_copy(send1.at[e, part], send1.at[e, part], s1.at[e]).wait()
+        pltpu.make_async_copy(send4.at[e, part], send4.at[e, part], s4.at[e]).wait()
+        pltpu.make_async_copy(recv4.at[e], recv4.at[e], r4.at[e]).wait()
         part = pl.ds(0, W - 64)
         pltpu.make_async_copy(send2.at[e, part], send2.at[e, part], s2.at[e]).wait()
         pltpu.make_async_copy(send3.at[e, part], send3.at[e, part], s3.at[e]).wait()
     for i in range(1, GROUPS):
         pltpu.make_async_copy(pg16.at[0], pg16.at[0], s5.at[i - 1]).wait()
         pltpu.make_async_copy(agr.at[0], agr.at[0], s6.at[i - 1]).wait()
-    pltpu.make_async_copy(send4.at[pl.ds(0, 127)], send4.at[pl.ds(0, 127)], s4).wait()
-    pltpu.make_async_copy(recv4, recv4, r4).wait()
 
 
 VMEM = pl.BlockSpec(memory_space=pltpu.VMEM)
 SMEM = pl.BlockSpec(memory_space=pltpu.SMEM)
 ANY = pl.BlockSpec(memory_space=pl.ANY)
-EXCHANGE = (DEVICES, PER, STRIPS, LANES)
+EXCHANGE = (PER, DEVICES, STRIPS, LANES)
 
 
 def local(spectrum, pupil, measured, offsets):
+    offsets = offsets.T
     small = pltpu.CompilerParams(vmem_limit_bytes=24 << 20)
     rows = spectrum.shape[1]
     tiles = spectrum.shape[3] // LANES
@@ -420,7 +429,8 @@
             pltpu.VMEM((4, 2 * Q, 2 * Q), BF16),
             pltpu.VMEM((4, 2 * Q, 2 * Q), BF16),
             pltpu.VMEM((4, Q, 2 * Q), BF16),
-            pltpu.VMEM(EXCHANGE, BF16),
+            pltpu.VMEM(EXCHANGE[1:], BF16),
+            pltpu.VMEM(EXCHANGE[1:], BF16),
             pltpu.VMEM((DEVICES, STRIPS, LANES), F32),
             pltpu.VMEM((DEVICES, STRIPS, LANES), F32),
             pltpu.VMEM((LANES, LANES), F32),
@@ -436,22 +446,26 @@
             pltpu.VMEM((4, 64, 2 * Q), F32),
             pltpu.VMEM((PER, W, LANES), BF16),
             pltpu.VMEM((PER, BLOCKS, 64, LANES), BF16),
-            pltpu.VMEM((PER, DEVICES, STRIPS, LANES), F32),
+            pltpu.VMEM((DEVICES, STRIPS, LANES), F32),
             pltpu.VMEM(EXCHANGE, BF16),
             pltpu.VMEM((W, LANES), F32),
             pltpu.VMEM((4, Q, LANES), BF16),
             pltpu.VMEM((4, Q, LANES), BF16),
             pltpu.VMEM((4, Q, LANES), BF16),
-            dma((4,)), dma, dma, dma((PER,)), dma((PER,)), dma((PER,)), dma((PER,)),
-            dma, dma, dma((3,)), dma, dma((3,)), dma,
+            dma((4,)), dma((PER,)), dma((PER,)), dma((PER,)), dma((PER,)), dma((PER,)), dma((PER,)),
+            dma((PER,)), dma((PER,)), dma((3,)), dma, dma((3,)), dma,
         ],
-        compiler_params=pltpu.CompilerParams(collective_id=0, has_side_effects=True, vmem_limit_bytes=58 << 20),
+        compiler_params=pltpu.CompilerParams(collective_id=0, has_side_effects=True, vmem_limit_bytes=48 << 20),
         name="core",
     )(offsets, send1, pup, meas, *(jnp.asarray(t) for t in tables()))
-    total = pl.pallas_call(
-        add_kernel, out_shape=jax.ShapeDtypeStruct(x.shape, F32), in_specs=[SMEM, VMEM], out_specs=VMEM,
-        compiler_params=small, name="add",
-    )(offsets, recv4)
+    total, pgrad = pl.pallas_call(
+        add_kernel,
+        out_shape=(jax.ShapeDtypeStruct(x.shape, F32), jax.ShapeDtypeStruct((LANES, W), F32)),
+        in_specs=[SMEM, VMEM, VMEM],
+        out_specs=(VMEM, VMEM),
+        compiler_params=small,
+        name="add",
+    )(offsets, recv4, pgrad)
     spec_grad = total.reshape(rows, tiles, 2, LANES).transpose(0, 2, 1, 3).reshape(spectrum.shape)
     return spec_grad, pgrad.reshape(2, 64, W).transpose(0, 2, 1)
 

time: 120 us -> 99.7 us (0.83)
  the two profiles are of different devices: /device:TPU:0 before, /device:TPU:28 now
where the time goes in v2:
time: 99.7 us; the launch traced here: 99.5 us
  Pallas kernels  96 us (96%)
  local copies, waits for them, and re-layouts  2.88 us (3%)
    pallas_call x1, Pallas kernels, local(): pl.pallas_call(core_kernel, out_shape=(jax.ShapeDtypeStruct(EXCHANGE, BF1...  86.1 us
    pallas_call x1, Pallas kernels, local(): pl.pallas_call(add_kernel, out_shape=(jax.ShapeDtypeStruct(x.shape, F32),...  6.89 us
    pallas_call x1, Pallas kernels, local(): pl.pallas_call(cut_kernel, out_shape=jax.ShapeDtypeStruct(EXCHANGE, BF16)...  2.96 us
    unnamed x10, local copies, waits for them, and re-layouts  2.88 us

profile of v2, /device:TPU:28, one launch (start us, length us, event | category | flops | bytes accessed | tf_op | source)
XLA Modules:
  0.0 99.5 jit_solution(6141706371698584740)
XLA Ops:
  0.6 0.0 copy-start.4
  0.6 0.0 copy-start
  0.7 2.2 %copy-done = f32[1,64,2,8192]{3,2,1,0:T(2,128)S(1)} copy-done((f32[1,64,2,8192]{3,2,1,0:T(2,128)S(1)}, f32[1,64,2,8192]{3,2,1,0:T(2,128)}, u32[]{:S(2)}) %copy-start) | copy-done | bytes 4194328
  2.8 0.0 copy-start.3
  2.8 0.7 copy-done.3
  3.5 0.0 copy-start.1
  3.5 0.0 copy-start.2
  3.5 3.0 %cut.1.send1 = bf16[2,128,16,128]{3,2,1,0:T(8,128)(2,1)S(1)} custom-call(s32[2,8]{1,0:T(2,128)S(1)} %bitcast.21, f32[8192,128]{1,0:T(8,128)S(1)} %bitcast.18), custom_call_target="tpu_custom_call" | custom-call | tf_op jit(solution)/shard_map/cut/pallas_call | solution.py:415
  6.5 0.0 copy-done.4
  6.5 0.0 copy-done.1
  6.5 0.0 copy-done.2
  6.5 86.1 %core.1 = (bf16[2,128,16,128]{3,2,1,0:T(8,128)(2,1)S(1)}, f32[128,2048]{1,0:T(8,128)S(1)}) custom-call(s32[2,8]{1,0:T(2,128)S(1)} %bitcast.22, bf16[2,128,16,128]{3,2,1,0:T(8,128)(2,1)S(1)} %cut.1.send1, f32[128,2048]{1,0:T(8,128)S(1)} %bitcast.19, f32[128,2048]{1,0:T(8,128)S(1)} %bitcast.20, bf16[4,512,1024]{2,1,0:T(8,128)(2,1)} %constant.8.clone.h1, ...), custom_call_target="tpu_custom_call" | custom-call | tf_op jit(solution)/shard_map/core/pallas_call | solution.py:422
  92.7 6.9 %add.1 = (f32[8192,128]{1,0:T(8,128)}, f32[128,2048]{1,0:T(8,128)}) custom-call(s32[2,8]{1,0:T(2,128)S(1)} %bitcast.23, bf16[2,128,16,128]{3,2,1,0:T(8,128)(2,1)S(1)} %get-tuple-element.6.terms, f32[128,2048]{1,0:T(8,128)S(1)} %get-tuple-element.7.pgrad), custom_call_target="tpu_custom_call" | custom-call | tf_op jit(solution)/shard_map/add/pallas_call | solution.py:461
Async XLA Ops:
  0.6 5.9 %copy-start.4 = (s32[8,2]{0,1:T(2,128)S(1)}, s32[8,2]{0,1:T(2,128)}, u32[]{:S(2)}) copy-start(s32[8,2]{0,1:T(2,128)} %param.11) | copy-start | bytes 196
  0.6 2.2 %copy-start = (f32[1,64,2,8192]{3,2,1,0:T(2,128)S(1)}, f32[1,64,2,8192]{3,2,1,0:T(2,128)}, u32[]{:S(2)}) copy-start(f32[1,64,2,8192]{3,2,1,0:T(2,128)} %param.8) | copy-start | bytes 12582916
  2.8 0.7 copy-start.3
  3.5 3.0 %copy-start.1 = (f32[2,2048,64]{1,2,0:T(8,128)S(1)}, f32[2,2048,64]{1,2,0:T(8,128)}, u32[]{:S(2)}) copy-start(f32[2,2048,64]{1,2,0:T(8,128)} %param.9) | copy-start | bytes 3145732
  3.5 3.0 %copy-start.2 = (f32[2,64,2048]{2,1,0:T(8,128)S(1)}, f32[2,64,2048]{2,1,0:T(8,128)}, u32[]{:S(2)}) copy-start(f32[2,64,2048]{2,1,0:T(8,128)} %param.10) | copy-start | bytes 3145732

commit v3 on v2

--- a/solution.py
+++ b/solution.py
@@ -19,6 +19,8 @@
 GROUPS = 4
 PER = 2
 LEDS = 8
+SPAN = 40
+PAD = 136
 STEP = 11
 MESH = pl.DeviceIdType.MESH
 F32 = jnp.float32
@@ -44,7 +46,9 @@
         c, s = c.reshape(8, 64, Q), s.reshape(8, 64, Q)
         re = np.concatenate([c, s], axis=2)
         im = np.concatenate([-s, c], axis=2)
-        both = np.stack([re, im], axis=1).reshape(2 * Q, 2 * Q)
+        both = np.stack([re, im], axis=1)
+        both[1::2] = both[1::2, ::-1]
+        both = both.reshape(2 * Q, 2 * Q)
         cols_fwd.append(both / W)
         cols_back.append(both.T)
     return tuple(np.stack(t).astype(ml_dtypes.bfloat16) for t in (rows_fwd, cols_fwd, cols_back, rows_back))
@@ -62,48 +66,58 @@
     return lax.axis_index("band"), lax.axis_index("led"), lax.axis_index("pencil")
 
 
-def cut_kernel(off, x, out):
+def cut_kernel(off, x, out, held, sem):
     band, led, pencil = position()
     me = band * 16 + led * 4 + pencil
     lane = lane_id(STRIPS)
     half = lane < 64
 
+    def start_of(l):
+        return pl.multiple_of(jnp.minimum(off[1, l] >> 9, 11) * 8, 8)
+
+    def fetch(l):
+        first = (off[0, l] - me + (DEVICES - 1)) >> 7
+        source = x.at[pl.ds(first, STRIPS), pl.ds(start_of(l), SPAN)]
+        return pltpu.make_async_copy(source, held.at[l], sem.at[l])
+
+    for l in range(LEDS):
+        fetch(l).start()
+
     def one(l, carry):
-        first = (off[0, l] - me + (DEVICES - 1)) >> 7
         col = off[1, l]
         tile, within = col >> 7, col & 127
-        keep = lane < LANES - within
-        turn = (LANES - within) & 127
+        keeps = (lane < LANES - within, (lane ^ 64) < LANES - within)
+        turns = ((LANES - within) & 127, (LANES + 64 - within) & 127)
+        fetch(l).wait()
 
         def load(k, part):
-            at = first * LANES + 2 * jnp.minimum(tile + k, 63) + part
-            return pltpu.roll(x[pl.ds(at, STRIPS, stride=LANES), :], turn, 1)
+            return pltpu.roll(held[l, :, 2 * jnp.minimum(tile + k, 63) + part - start_of(l), :], turns[part], 1)
 
         re, im = load(0, 0), load(0, 1)
         for k in range(16):
             next_re, next_im = load(k + 1, 0), load(k + 1, 1)
-            a = jnp.where(keep, re, next_re)
-            b = jnp.where(keep, im, next_im)
+            a = jnp.where(keeps[0], re, next_re)
+            b = jnp.where(keeps[1], im, next_im)
             slot = (l >> 1) * BLOCKS + 2 * k
-            out[l & 1, slot] = jnp.where(half, a, swap(b)).astype(BF16)
-            out[l & 1, slot + 1] = jnp.where(half, swap(a), b).astype(BF16)
+            out[l & 1, slot] = jnp.where(half, a, b).astype(BF16)
+            out[l & 1, slot + 1] = jnp.where(half, b, a).astype(BF16)
             re, im = next_re, next_im
         return carry
 
     lax.fori_loop(0, LEDS, one, 0)
 
 
-def add_kernel(off, terms, pgrad, out, pgrad_out):
+def add_kernel(off, terms, pgrad, out, pgrad_out, acc, sem):
     band, led, pencil = position()
     me = band * 16 + led * 4 + pencil
     lane = lane_id(STRIPS)
     half = lane < 64
 
     def clear(i, carry):
-        out[pl.ds(pl.multiple_of(i * 256, 256), 256), :] = jnp.zeros((256, LANES), F32)
+        acc[i] = jnp.zeros((PAD, LANES), F32)
         return carry
 
-    lax.fori_loop(0, out.shape[0] // 256, clear, 0)
+    lax.fori_loop(0, acc.shape[0], clear, 0)
     pgrad_out[...] = pgrad[...]
 
     def one(l, carry):
@@ -113,7 +127,7 @@
         low = lane < within
 
         def place(k, part):
-            return pl.ds(first * LANES + 2 * jnp.minimum(tile + k, 63) + part, STRIPS, stride=LANES)
+            return pl.ds(first, STRIPS), 2 * (tile + k) + part
 
         zero = jnp.zeros((STRIPS, LANES), F32)
         last = (zero, zero)
@@ -123,25 +137,32 @@
             a = terms[l & 1, slot].astype(F32)
             b = terms[l & 1, slot + 1].astype(F32)
             now = (
-                pltpu.roll(jnp.where(half, a, swap(b)), within, 1),
-                pltpu.roll(jnp.where(half, swap(a), b), within, 1),
+                pltpu.roll(jnp.where(half, a, b), within, 1),
+                pltpu.roll(jnp.where(half, b, a), within ^ 64, 1),
             )
-            values.append([out[place(k, p), :] + jnp.where(low, last[p], now[p]) for p in range(2)])
+            for p in range(2):
+                rows, at = place(k, p)
+                values.append(acc[rows, at, :] + jnp.where(low, last[p], now[p]))
             last = now
-        for k in range(16):
+        for p in range(2):
+            rows, at = place(16, p)
+            values.append(acc[rows, at, :] + jnp.where(low, last[p], zero))
+        for k in range(17):
             for p in range(2):
-                out[place(k, p), :] = values[k][p]
-        for p in range(2):
-            out[place(16, p), :] = out[place(16, p), :] + jnp.where(low, last[p], zero)
+                rows, at = place(k, p)
+                acc[rows, at, :] = values[2 * k + p]
         return carry
 
     lax.fori_loop(0, LEDS, one, 0)
+    done = pltpu.make_async_copy(acc.at[:, pl.ds(0, LANES)], out, sem)
+    done.start()
+    done.wait()
 
 
 def core_kernel(
     off, send1, pup, meas, h1, h2, h3, h4, recv4, pgout,
     t1, t2, t3, t4, recv1_0, recv1_1, pup_r, pup_i, tmp_r, tmp_i, perm, smq, x1, ys, send2, recv2, xq, rq, zs,
-    send3, recv3, wg, send4, pg, pg16, rsr, agr,
+    send3, recv3, wg, wo, send4, pg, pg16, rsr, agr,
     tsem, s1, r1, s2, r2, s3, r3, s4, r4, s5, r5, s6, r6,
 ):
     recv1 = (recv1_0, recv1_1)
@@ -149,7 +170,12 @@
     me = band * 16 + led * 4 + pencil
     block = band * 4 + pencil
     slot_me = led * BLOCKS + block
-    sgn = jnp.where(lane_id(1) < 64, -1.0, 1.0).astype(F32)
+    odd_pencil = pencil & 1
+
+    def sign(odd):
+        return jnp.where(((lane_id(1) >> 6) ^ odd) == 0, -1.0, 1.0).astype(F32)
+
+    sgn = sign(odd_pencil)
 
     def device(d):
         return {"band": d >> 4, "led": (d >> 2) & 3, "pencil": d & 3}
@@ -213,37 +239,47 @@
     def shift(e):
         return off[0, led * PER + e] & 127
 
-    def send_plane(src, dst, ssem, rsem):
+    def send_plane(b, src, dst, ssem, rsem):
+        pltpu.make_async_remote_copy(
+            src_ref=src.at[pl.ds(pl.multiple_of(b * 64, 64), 64)],
+            dst_ref=dst.at[block],
+            send_sem=ssem,
+            recv_sem=rsem,
+            device_id=plane(b),
+            device_id_type=MESH,
+        ).start()
+
+    def spread(work, src, dst, ssem, rsem):
+        def go(i, own):
+            at = (3 * i + block) & 7
+            work(at)
+            for k in range(1 if own else 0, 4):
+                send_plane(at + 8 * ((k + (block >> 3)) & 3), src, dst, ssem, rsem)
+
+        def step(i, c):
+            go(i, False)
+            return c
+
+        lax.fori_loop(1, 8, step, 0)
+        go(8, True)
         pltpu.make_async_copy(src.at[pl.ds(pl.multiple_of(block * 64, 64), 64)], dst.at[block], rsem).start()
-
-        def go(i, c):
-            b = (block + i * STEP) & 31
-            pltpu.make_async_remote_copy(
-                src_ref=src.at[pl.ds(pl.multiple_of(b * 64, 64), 64)],
-                dst_ref=dst.at[block],
-                send_sem=ssem,
-                recv_sem=rsem,
-                device_id=plane(b),
-                device_id_type=MESH,
-            ).start()
-            return c
-
-        lax.fori_loop(1, BLOCKS, go, 0)
 
     for e in range(PER):
         pltpu.make_async_copy(recv1[e], recv1[e], r1.at[e]).wait()
         delta = shift(e)
 
-        def product(w, c):
-            d = 4 * (w & 31) + (w >> 5)
-            win = recv1[e][(d + delta) & 127].astype(F32)
-            prod = win * pup_r[w] + swap(win) * pup_i[w]
-            at = pl.multiple_of((w & 31) * STRIPS, STRIPS)
-            x1[w >> 5, pl.ds(at, STRIPS), :] = prod.astype(BF16)
-            x1[w >> 5, pl.ds(at + Q, STRIPS), :] = (swap(prod) * sgn).astype(BF16)
-            return c
-
-        lax.fori_loop(0, DEVICES, product, 0, unroll=8)
+        def product(g, c):
+            d = 32 * (g & 3) + (g >> 2) + delta
+            win = jnp.concatenate([recv1[e][(d + 4 * k) & 127] for k in range(8)], axis=0).astype(F32)
+            pr = pup_r[pl.ds(8 * g, 8)].reshape(LANES, LANES)
+            pi = pup_i[pl.ds(8 * g, 8)].reshape(LANES, LANES)
+            other = swap(win)
+            at = pl.multiple_of((g & 3) * LANES, LANES)
+            x1[g >> 2, pl.ds(at, LANES), :] = (win * pr + other * pi).astype(BF16)
+            x1[g >> 2, pl.ds(at + Q, LANES), :] = ((other * pr - win * pi) * sgn).astype(BF16)
+            return c
+
+        lax.fori_loop(0, 16, product, 0)
 
         def first(v, c):
             ys[v] = jnp.dot(t1[v], x1[v], preferred_element_type=F32)
@@ -251,7 +287,7 @@
 
         lax.fori_loop(0, 4, first, 0)
 
-        def butterfly(i, c):
+        def butterfly(i):
             at = pl.multiple_of(i * 64, 64)
             rows = pl.ds(at, 64)
             y0, y1, y2, y3 = (ys[v, rows, :] for v in range(4))
@@ -259,10 +295,8 @@
             diff, turned = y0 - y2, swap(y1 - y3) * sgn
             for u, value in enumerate((even + odd, diff + turned, even - odd, diff - turned)):
                 send2[e, pl.ds(at + u * Q, 64), :] = value.astype(BF16)
-            return c
-
-        lax.fori_loop(0, 8, butterfly, 0)
-        send_plane(send2.at[e], recv2.at[e], s2.at[e], r2.at[e])
+
+        spread(butterfly, send2.at[e], recv2.at[e], s2.at[e], r2.at[e])
 
     fetch[1].wait()
     fetch[2].wait()
@@ -271,7 +305,7 @@
         for b in range(8):
             a0, a1, a2, a3 = (recv2[e, b + 8 * u].astype(F32) for u in range(4))
             even, odd = a0 + a2, a1 + a3
-            diff, turned = a0 - a2, swap(a1 - a3) * sgn
+            diff, turned = a0 - a2, swap(a1 - a3) * sign(b & 1)
             for q, value in enumerate((even + odd, diff + turned, even - odd, diff - turned)):
                 xq[q, :, b * LANES : (b + 1) * LANES] = value.astype(BF16)
 
@@ -285,13 +319,15 @@
             return c
 
         lax.fori_loop(0, 4, field, 0)
-        for b in range(8):
-            z0, z1, z2, z3 = (zs[q, :, b * LANES : (b + 1) * LANES] for q in range(4))
+        def combine(i):
+            lanes = pl.ds(pl.multiple_of(i * LANES, LANES), LANES)
+            z0, z1, z2, z3 = (zs[q, :, lanes] for q in range(4))
             even, odd = z0 + z2, z1 + z3
-            diff, turned = z0 - z2, swap(z1 - z3) * sgn
+            diff, turned = z0 - z2, swap(z1 - z3) * sign(i & 1)
             for u, value in enumerate((even + odd, diff - turned, even - odd, diff + turned)):
-                send3[e, (b + 8 * u) * 64 : (b + 8 * u + 1) * 64, :] = value.astype(BF16)
-        send_plane(send3.at[e], recv3.at[e], s3.at[e], r3.at[e])
+                send3[e, pl.ds(pl.multiple_of(i * 64, 64) + u * Q, 64), :] = value.astype(BF16)
+
+        spread(combine, send3.at[e], recv3.at[e], s3.at[e], r3.at[e])
 
     fetch[3].wait()
     def along(i):
@@ -304,11 +340,17 @@
         def fold(i, c):
             at = pl.multiple_of(i * 64, 64)
             a0, a1, a2, a3 = (recv3[e, i + 8 * u].astype(F32) for u in range(4))
-            even, odd = a0 + a2, a1 + a3
-            diff, turned = a0 - a2, swap(a1 - a3) * sgn
-            for q, value in enumerate((even + odd, diff - turned, even - odd, diff + turned)):
+            b0, b1, b2, b3 = (swap(a) for a in (a0, a1, a2, a3))
+            even, odd, diff, turned = a0 + a2, a1 + a3, a0 - a2, (b1 - b3) * sgn
+            back_even, back_odd, back_diff, back_turned = b0 + b2, b1 + b3, b0 - b2, (a1 - a3) * sgn
+            for q, (value, other) in enumerate((
+                (even + odd, back_even + back_odd),
+                (diff - turned, back_diff + back_turned),
+                (even - odd, back_even - back_odd),
+                (diff + turned, back_diff - back_turned),
+            )):
                 x1[q, pl.ds(at, 64), :] = value.astype(BF16)
-                x1[q, pl.ds(at + Q, 64), :] = (swap(value) * (-sgn)).astype(BF16)
+                x1[q, pl.ds(at + Q, 64), :] = (other * (-sgn)).astype(BF16)
             return c
 
         lax.fori_loop(0, 8, fold, 0)
@@ -316,53 +358,59 @@
         def last(q, c):
             got = jnp.dot(t4[q], x1[q], preferred_element_type=F32)
             wg[pl.ds(q * 32, 32)] = got.reshape(32, STRIPS, LANES)
+            wo[pl.ds(q * 32, 32)] = swap(got).reshape(32, STRIPS, LANES)
             return c
 
         lax.fori_loop(0, 4, last, 0)
 
-        def pupil_sum(w, c):
-            rows = pl.ds(pl.multiple_of(w * STRIPS, STRIPS), STRIPS)
-            d = 4 * (w & 31) + (w >> 5)
-            win = recv1[e][(d + delta) & 127].astype(F32)
-            grad = wg[w]
+        def pupil_sum(g, c):
+            rows = pl.ds(pl.multiple_of(g * LANES, LANES), LANES)
+            d = 32 * (g & 3) + (g >> 2) + delta
+            win = jnp.concatenate([recv1[e][(d + 4 * k) & 127] for k in range(8)], axis=0).astype(F32)
+            grad = wg[pl.ds(8 * g, 8)].reshape(LANES, LANES)
             other = swap(win)
-            half = lane_id(STRIPS) < 64
-            value = grad * jnp.where(half, win, other) - swap(grad) * (jnp.where(half, other, win) * sgn)
+            real = ((lane_id(LANES) >> 6) ^ odd_pencil) == 0
+            turned = wo[pl.ds(8 * g, 8)].reshape(LANES, LANES)
+            value = grad * jnp.where(real, win, other) - turned * (jnp.where(real, other, win) * sgn)
             if e == 0:
                 pg[rows, :] = value
             else:
                 value = value + pg[rows, :]
                 pg[rows, :] = value
-                pg16[w >> 5, pl.ds(pl.multiple_of((w & 31) * STRIPS, STRIPS), STRIPS), :] = value.astype(BF16)
-            return c
-
-        def term(d, c):
-            w0 = (d - delta) & 127
-            w = (w0 & 3) * 32 + (w0 >> 2)
-            grad = wg[w]
-            send4[e, d] = (grad * pup_r[w] - swap(grad) * pup_i[w]).astype(BF16)
-            return c
-
-        def start4(i, c):
-            d = (me + i * STEP) & 127
-            pltpu.make_async_remote_copy(
-                src_ref=send4.at[e, d], dst_ref=recv4.at[e, slot_me], send_sem=s4.at[e], recv_sem=r4.at[e],
-                device_id=device(d), device_id_type=MESH,
-            ).start()
+                pg16[g >> 2, pl.ds(pl.multiple_of((g & 3) * LANES, LANES), LANES), :] = value.astype(BF16)
+            return c
+
+        def term(g, own):
+            places = [(me + (8 * g + k + 1) * STEP) & 127 for k in range(8)]
+            values = []
+            for d in places:
+                w0 = (d - delta) & 127
+                w = (w0 & 3) * 32 + (w0 >> 2)
+                values.append((wg[w] * pup_r[w] - wo[w] * pup_i[w]).astype(BF16))
+            for d, value in zip(places, values):
+                send4[e, d] = value
+            for d in places[: 7 if own else 8]:
+                pltpu.make_async_remote_copy(
+                    src_ref=send4.at[e, d], dst_ref=recv4.at[e, slot_me], send_sem=s4.at[e], recv_sem=r4.at[e],
+                    device_id=device(d), device_id_type=MESH,
+                ).start()
+
+        def terms(g, c):
+            term(g, False)
             return c
 
         if e > 0:
-            lax.fori_loop(0, DEVICES, pupil_sum, 0, unroll=8)
+            lax.fori_loop(0, 16, pupil_sum, 0)
             for i in range(1, GROUPS):
                 pltpu.make_async_remote_copy(
                     src_ref=pg16.at[(led + i) & 3], dst_ref=rsr.at[led], send_sem=s5.at[i - 1], recv_sem=r5,
                     device_id=along(i), device_id_type=MESH,
                 ).start()
-        lax.fori_loop(0, DEVICES, term, 0, unroll=8)
+        lax.fori_loop(0, 15, terms, 0)
+        term(15, True)
         pltpu.make_async_copy(send4.at[e, me], recv4.at[e, slot_me], r4.at[e]).start()
-        lax.fori_loop(1, DEVICES, start4, 0)
         if e == 0:
-            lax.fori_loop(0, DEVICES, pupil_sum, 0, unroll=8)
+            lax.fori_loop(0, 16, pupil_sum, 0)
 
     pltpu.make_async_copy(rsr.at[pl.ds(0, 3)], rsr.at[pl.ds(0, 3)], r5).wait()
     total = pg[pl.ds(pl.multiple_of(led * Q, Q), Q), :]
@@ -382,7 +430,10 @@
     def back(s, c):
         for v in range(4):
             tmp_r[pl.ds(v, 32, stride=4), :] = pg[pl.ds(v * Q + s, 32, stride=STRIPS), :]
-        pgout[:, pl.ds(pl.multiple_of(s * LANES, LANES), LANES)] = tmp_r[...].T
+        got = tmp_r[...].T
+        lanes = pl.ds(pl.multiple_of(s * LANES, LANES), LANES)
+        pgout[:64, lanes] = jnp.where(odd_pencil == 0, got[:64], got[64:])
+        pgout[64:, lanes] = jnp.where(odd_pencil == 0, got[64:], got[:64])
         return c
 
     lax.fori_loop(0, STRIPS, back, 0)
@@ -403,6 +454,7 @@
 VMEM = pl.BlockSpec(memory_space=pltpu.VMEM)
 SMEM = pl.BlockSpec(memory_space=pltpu.SMEM)
 ANY = pl.BlockSpec(memory_space=pl.ANY)
+HBM = pl.BlockSpec(memory_space=pltpu.HBM)
 EXCHANGE = (PER, DEVICES, STRIPS, LANES)
 
 
@@ -411,14 +463,19 @@
     small = pltpu.CompilerParams(vmem_limit_bytes=24 << 20)
     rows = spectrum.shape[1]
     tiles = spectrum.shape[3] // LANES
-    x = spectrum.reshape(rows, 2, tiles, LANES).transpose(0, 2, 1, 3).reshape(rows * tiles * 2, LANES)
+    dma = pltpu.SemaphoreType.DMA
+    x = spectrum.reshape(rows, 2, tiles, LANES).transpose(0, 2, 1, 3).reshape(rows, 2 * tiles, LANES)
     send1 = pl.pallas_call(
-        cut_kernel, out_shape=jax.ShapeDtypeStruct(EXCHANGE, BF16), in_specs=[SMEM, VMEM], out_specs=VMEM,
-        compiler_params=small, name="cut",
+        cut_kernel,
+        out_shape=jax.ShapeDtypeStruct(EXCHANGE, BF16),
+        in_specs=[SMEM, HBM],
+        out_specs=VMEM,
+        scratch_shapes=[pltpu.VMEM((LEDS, STRIPS, SPAN, LANES), F32), dma((LEDS,))],
+        compiler_params=pltpu.CompilerParams(vmem_limit_bytes=60 << 20),
+        name="cut",
     )(offsets, x)
     pup = pupil.transpose(0, 2, 1).reshape(LANES, W)
     meas = measured.reshape(PER * 64, W)
-    dma = pltpu.SemaphoreType.DMA
     recv4, pgrad = pl.pallas_call(
         core_kernel,
         out_shape=(jax.ShapeDtypeStruct(EXCHANGE, BF16), jax.ShapeDtypeStruct((LANES, W), F32)),
@@ -447,6 +504,7 @@
             pltpu.VMEM((PER, W, LANES), BF16),
             pltpu.VMEM((PER, BLOCKS, 64, LANES), BF16),
             pltpu.VMEM((DEVICES, STRIPS, LANES), F32),
+            pltpu.VMEM((DEVICES, STRIPS, LANES), F32),
             pltpu.VMEM(EXCHANGE, BF16),
             pltpu.VMEM((W, LANES), F32),
             pltpu.VMEM((4, Q, LANES), BF16),
@@ -462,7 +520,8 @@
         add_kernel,
         out_shape=(jax.ShapeDtypeStruct(x.shape, F32), jax.ShapeDtypeStruct((LANES, W), F32)),
         in_specs=[SMEM, VMEM, VMEM],
-        out_specs=(VMEM, VMEM),
+        out_specs=(HBM, VMEM),
+        scratch_shapes=[pltpu.VMEM((rows, PAD, LANES), F32), dma],
         compiler_params=small,
         name="add",
     )(offsets, recv4, pgrad)

time: 99.7 us -> 96 us (0.963)
  the two profiles are of different devices: /device:TPU:28 before, /device:TPU:0 now
where the time goes in v3:
time: 96 us; the launch traced here: 95.4 us
  Pallas kernels  93.5 us (97%)
  local copies, waits for them, and re-layouts  1.23 us (1%)
    pallas_call x1, Pallas kernels, local(): pl.pallas_call(core_kernel, out_shape=(jax.ShapeDtypeStruct(EXCHANGE, BF1...  81.9 us
    pallas_call x1, Pallas kernels, local(): pl.pallas_call(add_kernel, out_shape=(jax.ShapeDtypeStruct(x.shape, F32),...  6.64 us
    pallas_call x1, Pallas kernels, local(): pl.pallas_call(cut_kernel, out_shape=jax.ShapeDtypeStruct(EXCHANGE, BF16)...  4.9 us

profile of v3, /device:TPU:0, one launch (start us, length us, event | category | flops | bytes accessed | tf_op | source)
XLA Modules:
  0.0 95.4 jit_solution(13291354790530358687)
XLA Ops:
  0.6 0.0 copy-start.3
  0.6 0.0 copy-start.2
  0.7 0.0 copy-start.1
  0.7 4.9 %cut.1.send1 = bf16[2,128,16,128]{3,2,1,0:T(8,128)(2,1)} custom-call(s32[2,8]{1,0:T(2,128)} %bitcast.20, f32[64,128,128]{2,1,0:T(8,128)} %bitcast.23), custom_call_target="tpu_custom_call" | custom-call | tf_op jit(solution)/shard_map/cut/pallas_call | solution.py:468
  5.6 0.0 copy-done.3
  5.6 0.0 copy-done.2
  5.6 0.0 copy-done.1
  5.6 0.0 copy-start
  5.6 1.2 %copy-done = bf16[2,128,16,128]{3,2,1,0:T(8,128)(2,1)S(1)} copy-done((bf16[2,128,16,128]{3,2,1,0:T(8,128)(2,1)S(1)}, bf16[2,128,16,128]{3,2,1,0:T(8,128)(2,1)}, u32[]{:S(2)}) %copy-start) | copy-done | bytes 1048600
  6.8 81.9 %core.1 = (bf16[2,128,16,128]{3,2,1,0:T(8,128)(2,1)S(1)}, f32[128,2048]{1,0:T(8,128)S(1)}) custom-call(s32[2,8]{1,0:T(2,128)S(1)} %bitcast.21, bf16[2,128,16,128]{3,2,1,0:T(8,128)(2,1)S(1)} %copy-done, f32[128,2048]{1,0:T(8,128)S(1)} %bitcast.18, f32[128,2048]{1,0:T(8,128)S(1)} %bitcast.19, bf16[4,512,1024]{2,1,0:T(8,128)(2,1)} %constant.8.clone.h1, ...), custom_call_target="tpu_custom_call" | custom-call | tf_op jit(solution)/shard_map/core/pallas_call | solution.py:479
  88.8 6.6 %add.1 = (f32[64,128,128]{2,1,0:T(8,128)}, f32[128,2048]{1,0:T(8,128)}) custom-call(s32[2,8]{1,0:T(2,128)S(1)} %bitcast.22, bf16[2,128,16,128]{3,2,1,0:T(8,128)(2,1)S(1)} %get-tuple-element.6.terms, f32[128,2048]{1,0:T(8,128)S(1)} %get-tuple-element.7.pgrad), custom_call_target="tpu_custom_call" | custom-call | tf_op jit(solution)/shard_map/add/pallas_call | solution.py:519
Async XLA Ops:
  0.6 4.9 %copy-start.3 = (s32[8,2]{0,1:T(2,128)S(1)}, s32[8,2]{0,1:T(2,128)}, u32[]{:S(2)}) copy-start(s32[8,2]{0,1:T(2,128)} %param.11) | copy-start | bytes 196
  0.6 4.9 %copy-start.2 = (f32[2,64,2048]{2,1,0:T(8,128)S(1)}, f32[2,64,2048]{2,1,0:T(8,128)}, u32[]{:S(2)}) copy-start(f32[2,64,2048]{2,1,0:T(8,128)} %param.10) | copy-start | bytes 3145732
  0.7 4.9 %copy-start.1 = (f32[2,2048,64]{1,2,0:T(8,128)S(1)}, f32[2,2048,64]{1,2,0:T(8,128)}, u32[]{:S(2)}) copy-start(f32[2,2048,64]{1,2,0:T(8,128)} %param.9) | copy-start | bytes 3145732
  5.6 1.2 %copy-start = (bf16[2,128,16,128]{3,2,1,0:T(8,128)(2,1)S(1)}, bf16[2,128,16,128]{3,2,1,0:T(8,128)(2,1)}, u32[]{:S(2)}) copy-start(bf16[2,128,16,128]{3,2,1,0:T(8,128)(2,1)} %cut.1.send1) | copy-start | bytes 3145732

commit v4 on v3

--- a/solution.py
+++ b/solution.py
@@ -19,9 +19,8 @@
 GROUPS = 4
 PER = 2
 LEDS = 8
-SPAN = 40
 PAD = 136
-STEP = 11
+STEP = 27
 MESH = pl.DeviceIdType.MESH
 F32 = jnp.float32
 BF16 = jnp.bfloat16
@@ -66,32 +65,21 @@
     return lax.axis_index("band"), lax.axis_index("led"), lax.axis_index("pencil")
 
 
-def cut_kernel(off, x, out, held, sem):
+def cut_kernel(off, x, out):
     band, led, pencil = position()
     me = band * 16 + led * 4 + pencil
     lane = lane_id(STRIPS)
     half = lane < 64
 
-    def start_of(l):
-        return pl.multiple_of(jnp.minimum(off[1, l] >> 9, 11) * 8, 8)
-
-    def fetch(l):
+    def one(l, carry):
         first = (off[0, l] - me + (DEVICES - 1)) >> 7
-        source = x.at[pl.ds(first, STRIPS), pl.ds(start_of(l), SPAN)]
-        return pltpu.make_async_copy(source, held.at[l], sem.at[l])
-
-    for l in range(LEDS):
-        fetch(l).start()
-
-    def one(l, carry):
         col = off[1, l]
         tile, within = col >> 7, col & 127
         keeps = (lane < LANES - within, (lane ^ 64) < LANES - within)
         turns = ((LANES - within) & 127, (LANES + 64 - within) & 127)
-        fetch(l).wait()
 
         def load(k, part):
-            return pltpu.roll(held[l, :, 2 * jnp.minimum(tile + k, 63) + part - start_of(l), :], turns[part], 1)
+            return pltpu.roll(x[pl.ds(first, STRIPS), 2 * jnp.minimum(tile + k, 63) + part, :], turns[part], 1)
 
         re, im = load(0, 0), load(0, 1)
         for k in range(16):
@@ -107,7 +95,7 @@
     lax.fori_loop(0, LEDS, one, 0)
 
 
-def add_kernel(off, terms, pgrad, out, pgrad_out, acc, sem):
+def add_kernel(off, terms, pgrad, out, pgrad_out, acc, order, sem):
     band, led, pencil = position()
     me = band * 16 + led * 4 + pencil
     lane = lane_id(STRIPS)
@@ -120,8 +108,22 @@
     lax.fori_loop(0, acc.shape[0], clear, 0)
     pgrad_out[...] = pgrad[...]
 
-    def one(l, carry):
+    for l in range(LEDS):
+        rank = jnp.int32(0)
+        for m in range(LEDS):
+            if m != l:
+                ahead = off[0, m] <= off[0, l] if m < l else off[0, m] < off[0, l]
+                rank = rank + ahead.astype(jnp.int32)
+        order[rank] = l
+
+    def leave(row, carry):
+        pltpu.make_async_copy(acc.at[row, pl.ds(0, LANES)], out.at[row], sem).start()
+        return carry
+
+    def one(i, gone):
+        l = order[i]
         first = (off[0, l] - me + (DEVICES - 1)) >> 7
+        lax.fori_loop(gone, first, leave, 0)
         col = off[1, l]
         tile, within = col >> 7, col & 127
         low = lane < within
@@ -151,18 +153,17 @@
             for p in range(2):
                 rows, at = place(k, p)
                 acc[rows, at, :] = values[2 * k + p]
-        return carry
-
-    lax.fori_loop(0, LEDS, one, 0)
-    done = pltpu.make_async_copy(acc.at[:, pl.ds(0, LANES)], out, sem)
-    done.start()
-    done.wait()
+        return first
+
+    gone = lax.fori_loop(0, LEDS, one, jnp.int32(0))
+    lax.fori_loop(gone, acc.shape[0], leave, 0)
+    pltpu.make_async_copy(acc.at[:, pl.ds(0, LANES)], out, sem).wait()
 
 
 def core_kernel(
     off, send1, pup, meas, h1, h2, h3, h4, recv4, pgout,
     t1, t2, t3, t4, recv1_0, recv1_1, pup_r, pup_i, tmp_r, tmp_i, perm, smq, x1, ys, send2, recv2, xq, rq, zs,
-    send3, recv3, wg, wo, send4, pg, pg16, rsr, agr,
+    send3, recv3, wg, wo, send4, pg, pgn, pg16, rsr, agr,
     tsem, s1, r1, s2, r2, s3, r3, s4, r4, s5, r5, s6, r6,
 ):
     recv1 = (recv1_0, recv1_1)
@@ -251,7 +252,7 @@
 
     def spread(work, src, dst, ssem, rsem):
         def go(i, own):
-            at = (3 * i + block) & 7
+            at = (5 * i + block) & 7
             work(at)
             for k in range(1 if own else 0, 4):
                 send_plane(at + 8 * ((k + (block >> 3)) & 3), src, dst, ssem, rsem)
@@ -375,9 +376,15 @@
             if e == 0:
                 pg[rows, :] = value
             else:
-                value = value + pg[rows, :]
-                pg[rows, :] = value
-                pg16[g >> 2, pl.ds(pl.multiple_of((g & 3) * LANES, LANES), LANES), :] = value.astype(BF16)
+                value = (value + pg[rows, :]).reshape(8, STRIPS, LANES)
+                for k in range(8):
+                    pgn[pl.ds(32 * (g & 3) + 4 * k + (g >> 2), STRIPS, stride=LANES), :] = value[k]
+            return c
+
+        def narrow(g, c):
+            pg16[g >> 1, pl.ds(pl.multiple_of((g & 1) * 256, 256), 256), :] = pgn[
+                pl.ds(pl.multiple_of(g * 256, 256), 256), :
+            ].astype(BF16)
             return c
 
         def term(g, own):
@@ -401,6 +408,7 @@
 
         if e > 0:
             lax.fori_loop(0, 16, pupil_sum, 0)
+            lax.fori_loop(0, 8, narrow, 0)
             for i in range(1, GROUPS):
                 pltpu.make_async_remote_copy(
                     src_ref=pg16.at[(led + i) & 3], dst_ref=rsr.at[led], send_sem=s5.at[i - 1], recv_sem=r5,
@@ -413,10 +421,14 @@
             lax.fori_loop(0, 16, pupil_sum, 0)
 
     pltpu.make_async_copy(rsr.at[pl.ds(0, 3)], rsr.at[pl.ds(0, 3)], r5).wait()
-    total = pg[pl.ds(pl.multiple_of(led * Q, Q), Q), :]
-    for i in range(1, GROUPS):
-        total = total + rsr[(led + i) & 3].astype(F32)
-    agr[led] = total.astype(BF16)
+    for k in range(4):
+        total = pgn[pl.ds(pl.multiple_of(led * Q + k * LANES, LANES), LANES), :]
+        for i in range(1, GROUPS):
+            total = total + rsr[(led + i) & 3, k * LANES : (k + 1) * LANES, :].astype(F32)
+        total = total.T
+        lanes = slice(k * LANES, (k + 1) * LANES)
+        agr[led, :64, lanes] = jnp.where(odd_pencil == 0, total[:64], total[64:]).astype(BF16)
+        agr[led, 64:, lanes] = jnp.where(odd_pencil == 0, total[64:], total[:64]).astype(BF16)
     for i in range(1, GROUPS):
         pltpu.make_async_remote_copy(
             src_ref=agr.at[led], dst_ref=agr.at[led], send_sem=s6.at[i - 1], recv_sem=r6,
@@ -425,18 +437,7 @@
     pltpu.make_async_copy(agr.at[pl.ds(0, 3)], agr.at[pl.ds(0, 3)], r6).wait()
 
     for v in range(4):
-        pg[v * Q : (v + 1) * Q, :] = agr[v].astype(F32)
-
-    def back(s, c):
-        for v in range(4):
-            tmp_r[pl.ds(v, 32, stride=4), :] = pg[pl.ds(v * Q + s, 32, stride=STRIPS), :]
-        got = tmp_r[...].T
-        lanes = pl.ds(pl.multiple_of(s * LANES, LANES), LANES)
-        pgout[:64, lanes] = jnp.where(odd_pencil == 0, got[:64], got[64:])
-        pgout[64:, lanes] = jnp.where(odd_pencil == 0, got[64:], got[:64])
-        return c
-
-    lax.fori_loop(0, STRIPS, back, 0)
+        pgout[:, v * Q : (v + 1) * Q] = agr[v].astype(F32)
 
     for e in range(PER):
         part = pl.ds(0, DEVICES - 1)
@@ -468,10 +469,9 @@
     send1 = pl.pallas_call(
         cut_kernel,
         out_shape=jax.ShapeDtypeStruct(EXCHANGE, BF16),
-        in_specs=[SMEM, HBM],
+        in_specs=[SMEM, VMEM],
         out_specs=VMEM,
-        scratch_shapes=[pltpu.VMEM((LEDS, STRIPS, SPAN, LANES), F32), dma((LEDS,))],
-        compiler_params=pltpu.CompilerParams(vmem_limit_bytes=60 << 20),
+        compiler_params=small,
         name="cut",
     )(offsets, x)
     pup = pupil.transpose(0, 2, 1).reshape(LANES, W)
@@ -507,9 +507,10 @@
             pltpu.VMEM((DEVICES, STRIPS, LANES), F32),
             pltpu.VMEM(EXCHANGE, BF16),
             pltpu.VMEM((W, LANES), F32),
+            pltpu.VMEM((W, LANES), F32),
             pltpu.VMEM((4, Q, LANES), BF16),
             pltpu.VMEM((4, Q, LANES), BF16),
-            pltpu.VMEM((4, Q, LANES), BF16),
+            pltpu.VMEM((4, LANES, Q), BF16),
             dma((4,)), dma((PER,)), dma((PER,)), dma((PER,)), dma((PER,)), dma((PER,)), dma((PER,)),
             dma((PER,)), dma((PER,)), dma((3,)), dma, dma((3,)), dma,
         ],
@@ -521,7 +522,7 @@
         out_shape=(jax.ShapeDtypeStruct(x.shape, F32), jax.ShapeDtypeStruct((LANES, W), F32)),
         in_specs=[SMEM, VMEM, VMEM],
         out_specs=(HBM, VMEM),
-        scratch_shapes=[pltpu.VMEM((rows, PAD, LANES), F32), dma],
+        scratch_shapes=[pltpu.VMEM((rows, PAD, LANES), F32), pltpu.SMEM((LEDS,), jnp.int32), dma],
         compiler_params=small,
         name="add",
     )(offsets, recv4, pgrad)

time: 96 us -> 91.2 us (0.950)
  Pallas kernels: 93.5 us -> 87.5 us
  local copies, waits for them, and re-layouts: 1.23 us -> 2.88 us
    pallas_call x1, Pallas kernels: 81.9 us -> 79.2 us  [local(): pl.pallas_call(core_kernel, out_shape=(jax.ShapeDtypeStruct(EXCHANGE, BF1...]
    pallas_call x1, Pallas kernels: 4.9 us -> 2.39 us  [local(): pl.pallas_call(cut_kernel, out_shape=jax.ShapeDtypeStruct(EXCHANGE, BF16)...]
    unnamed x8 -> x10, local copies, waits for them, and re-layouts: 1.23 us -> 2.88 us
where the time goes in v4:
time: 91.2 us; the launch traced here: 91.1 us
  Pallas kernels  87.5 us (96%)
  local copies, waits for them, and re-layouts  2.88 us (3%)
    pallas_call x1, Pallas kernels, local(): pl.pallas_call(core_kernel, out_shape=(jax.ShapeDtypeStruct(EXCHANGE, BF1...  79.2 us
    pallas_call x1, Pallas kernels, local(): pl.pallas_call(add_kernel, out_shape=(jax.ShapeDtypeStruct(x.shape, F32),...  5.95 us
    unnamed x10, local copies, waits for them, and re-layouts  2.88 us
    pallas_call x1, Pallas kernels, local(): pl.pallas_call(cut_kernel, out_shape=jax.ShapeDtypeStruct(EXCHANGE, BF16)...  2.39 us

profile of v4, /device:TPU:0, one launch (start us, length us, event | category | flops | bytes accessed | tf_op | source)
XLA Modules:
  0.0 91.1 jit_solution(13549352741420571538)
XLA Ops:
  0.6 0.0 copy-start.4
  0.6 0.0 copy-start
  0.7 2.2 %copy-done = f32[1,64,2,8192]{3,2,1,0:T(2,128)S(1)} copy-done((f32[1,64,2,8192]{3,2,1,0:T(2,128)S(1)}, f32[1,64,2,8192]{3,2,1,0:T(2,128)}, u32[]{:S(2)}) %copy-start) | copy-done | bytes 4194328
  2.8 0.0 copy-start.3
  2.8 0.7 copy-done.3
  3.5 0.0 copy-start.1
  3.5 0.0 copy-start.2
  3.5 2.4 %cut.1.send1 = bf16[2,128,16,128]{3,2,1,0:T(8,128)(2,1)S(1)} custom-call(s32[2,8]{1,0:T(2,128)S(1)} %bitcast.21, f32[64,128,128]{2,1,0:T(8,128)S(1)} %bitcast.18), custom_call_target="tpu_custom_call" | custom-call | tf_op jit(solution)/shard_map/cut/pallas_call | solution.py:469
  5.9 0.0 copy-done.4
  5.9 0.0 copy-done.1
  5.9 0.0 copy-done.2
  5.9 79.2 %core.1 = (bf16[2,128,16,128]{3,2,1,0:T(8,128)(2,1)S(1)}, f32[128,2048]{1,0:T(8,128)S(1)}) custom-call(s32[2,8]{1,0:T(2,128)S(1)} %bitcast.22, bf16[2,128,16,128]{3,2,1,0:T(8,128)(2,1)S(1)} %cut.1.send1, f32[128,2048]{1,0:T(8,128)S(1)} %bitcast.19, f32[128,2048]{1,0:T(8,128)S(1)} %bitcast.20, bf16[4,512,1024]{2,1,0:T(8,128)(2,1)} %constant.8.clone.h1, ...), custom_call_target="tpu_custom_call" | custom-call | tf_op jit(solution)/shard_map/core/pallas_call | solution.py:479
  85.1 6.0 %add.1 = (f32[64,128,128]{2,1,0:T(8,128)}, f32[128,2048]{1,0:T(8,128)}) custom-call(s32[2,8]{1,0:T(2,128)S(1)} %bitcast.23, bf16[2,128,16,128]{3,2,1,0:T(8,128)(2,1)S(1)} %get-tuple-element.6.terms, f32[128,2048]{1,0:T(8,128)S(1)} %get-tuple-element.7.pgrad), custom_call_target="tpu_custom_call" | custom-call | tf_op jit(solution)/shard_map/add/pallas_call | solution.py:520
Async XLA Ops:
  0.6 5.3 %copy-start.4 = (s32[8,2]{0,1:T(2,128)S(1)}, s32[8,2]{0,1:T(2,128)}, u32[]{:S(2)}) copy-start(s32[8,2]{0,1:T(2,128)} %param.11) | copy-start | bytes 196
  0.6 2.2 %copy-start = (f32[1,64,2,8192]{3,2,1,0:T(2,128)S(1)}, f32[1,64,2,8192]{3,2,1,0:T(2,128)}, u32[]{:S(2)}) copy-start(f32[1,64,2,8192]{3,2,1,0:T(2,128)} %param.8) | copy-start | bytes 12582916
  2.8 0.7 copy-start.3
  3.5 2.4 %copy-start.1 = (f32[2,2048,64]{1,2,0:T(8,128)S(1)}, f32[2,2048,64]{1,2,0:T(8,128)}, u32[]{:S(2)}) copy-start(f32[2,2048,64]{1,2,0:T(8,128)} %param.9) | copy-start | bytes 3145732
  3.5 2.4 %copy-start.2 = (f32[2,64,2048]{2,1,0:T(8,128)S(1)}, f32[2,64,2048]{2,1,0:T(8,128)}, u32[]{:S(2)}) copy-start(f32[2,64,2048]{2,1,0:T(8,128)} %param.10) | copy-start | bytes 3145732

commit v5 on v4

--- a/solution.py
+++ b/solution.py
@@ -280,13 +280,13 @@
             x1[g >> 2, pl.ds(at + Q, LANES), :] = ((other * pr - win * pi) * sgn).astype(BF16)
             return c
 
-        lax.fori_loop(0, 16, product, 0)
+        lax.fori_loop(0, 16, product, 0, unroll=2)
 
         def first(v, c):
             ys[v] = jnp.dot(t1[v], x1[v], preferred_element_type=F32)
             return c
 
-        lax.fori_loop(0, 4, first, 0)
+        lax.fori_loop(0, 4, first, 0, unroll=2)
 
         def butterfly(i):
             at = pl.multiple_of(i * 64, 64)
@@ -362,7 +362,7 @@
             wo[pl.ds(q * 32, 32)] = swap(got).reshape(32, STRIPS, LANES)
             return c
 
-        lax.fori_loop(0, 4, last, 0)
+        lax.fori_loop(0, 4, last, 0, unroll=2)
 
         def pupil_sum(g, c):
             rows = pl.ds(pl.multiple_of(g * LANES, LANES), LANES)
@@ -407,7 +407,7 @@
             return c
 
         if e > 0:
-            lax.fori_loop(0, 16, pupil_sum, 0)
+            lax.fori_loop(0, 16, pupil_sum, 0, unroll=2)
             lax.fori_loop(0, 8, narrow, 0)
             for i in range(1, GROUPS):
                 pltpu.make_async_remote_copy(
@@ -418,7 +418,7 @@
         term(15, True)
         pltpu.make_async_copy(send4.at[e, me], recv4.at[e, slot_me], r4.at[e]).start()
         if e == 0:
-            lax.fori_loop(0, 16, pupil_sum, 0)
+            lax.fori_loop(0, 16, pupil_sum, 0, unroll=2)
 
     pltpu.make_async_copy(rsr.at[pl.ds(0, 3)], rsr.at[pl.ds(0, 3)], r5).wait()
     for k in range(4):

time: 91.2 us -> 89 us (0.976)
  Pallas kernels: 87.5 us -> 85.3 us
    pallas_call x1, Pallas kernels: 79.2 us -> 76.9 us  [local(): pl.pallas_call(core_kernel, out_shape=(jax.ShapeDtypeStruct(EXCHANGE, BF1...]
where the time goes in v5:
time: 89 us; the launch traced here: 88.9 us
  Pallas kernels  85.3 us (96%)
  local copies, waits for them, and re-layouts  2.88 us (3%)
    pallas_call x1, Pallas kernels, local(): pl.pallas_call(core_kernel, out_shape=(jax.ShapeDtypeStruct(EXCHANGE, BF1...  76.9 us
    pallas_call x1, Pallas kernels, local(): pl.pallas_call(add_kernel, out_shape=(jax.ShapeDtypeStruct(x.shape, F32),...  6.03 us
    unnamed x10, local copies, waits for them, and re-layouts  2.88 us
    pallas_call x1, Pallas kernels, local(): pl.pallas_call(cut_kernel, out_shape=jax.ShapeDtypeStruct(EXCHANGE, BF16)...  2.39 us

profile of v5, /device:TPU:0, one launch (start us, length us, event | category | flops | bytes accessed | tf_op | source)
XLA Modules:
  0.0 88.9 jit_solution(5972962895958567857)
XLA Ops:
  0.6 0.0 copy-start.4
  0.6 0.0 copy-start
  0.7 2.2 %copy-done = f32[1,64,2,8192]{3,2,1,0:T(2,128)S(1)} copy-done((f32[1,64,2,8192]{3,2,1,0:T(2,128)S(1)}, f32[1,64,2,8192]{3,2,1,0:T(2,128)}, u32[]{:S(2)}) %copy-start) | copy-done | bytes 4194328
  2.8 0.0 copy-start.3
  2.8 0.7 copy-done.3
  3.5 0.0 copy-start.1
  3.5 0.0 copy-start.2
  3.5 2.4 %cut.1.send1 = bf16[2,128,16,128]{3,2,1,0:T(8,128)(2,1)S(1)} custom-call(s32[2,8]{1,0:T(2,128)S(1)} %bitcast.21, f32[64,128,128]{2,1,0:T(8,128)S(1)} %bitcast.18), custom_call_target="tpu_custom_call" | custom-call | tf_op jit(solution)/shard_map/cut/pallas_call | solution.py:469
  5.9 0.0 copy-done.4
  5.9 0.0 copy-done.1
  5.9 0.0 copy-done.2
  5.9 76.9 %core.1 = (bf16[2,128,16,128]{3,2,1,0:T(8,128)(2,1)S(1)}, f32[128,2048]{1,0:T(8,128)S(1)}) custom-call(s32[2,8]{1,0:T(2,128)S(1)} %bitcast.22, bf16[2,128,16,128]{3,2,1,0:T(8,128)(2,1)S(1)} %cut.1.send1, f32[128,2048]{1,0:T(8,128)S(1)} %bitcast.19, f32[128,2048]{1,0:T(8,128)S(1)} %bitcast.20, bf16[4,512,1024]{2,1,0:T(8,128)(2,1)} %constant.8.clone.h1, ...), custom_call_target="tpu_custom_call" | custom-call | tf_op jit(solution)/shard_map/core/pallas_call | solution.py:479
  82.9 6.0 %add.1 = (f32[64,128,128]{2,1,0:T(8,128)}, f32[128,2048]{1,0:T(8,128)}) custom-call(s32[2,8]{1,0:T(2,128)S(1)} %bitcast.23, bf16[2,128,16,128]{3,2,1,0:T(8,128)(2,1)S(1)} %get-tuple-element.6.terms, f32[128,2048]{1,0:T(8,128)S(1)} %get-tuple-element.7.pgrad), custom_call_target="tpu_custom_call" | custom-call | tf_op jit(solution)/shard_map/add/pallas_call | solution.py:520
Async XLA Ops:
  0.6 5.3 %copy-start.4 = (s32[8,2]{0,1:T(2,128)S(1)}, s32[8,2]{0,1:T(2,128)}, u32[]{:S(2)}) copy-start(s32[8,2]{0,1:T(2,128)} %param.11) | copy-start | bytes 196
  0.6 2.2 %copy-start = (f32[1,64,2,8192]{3,2,1,0:T(2,128)S(1)}, f32[1,64,2,8192]{3,2,1,0:T(2,128)}, u32[]{:S(2)}) copy-start(f32[1,64,2,8192]{3,2,1,0:T(2,128)} %param.8) | copy-start | bytes 12582916
  2.8 0.7 copy-start.3
  3.5 2.4 %copy-start.1 = (f32[2,2048,64]{1,2,0:T(8,128)S(1)}, f32[2,2048,64]{1,2,0:T(8,128)}, u32[]{:S(2)}) copy-start(f32[2,2048,64]{1,2,0:T(8,128)} %param.9) | copy-start | bytes 3145732
  3.5 2.4 %copy-start.2 = (f32[2,64,2048]{2,1,0:T(8,128)S(1)}, f32[2,64,2048]{2,1,0:T(8,128)}, u32[]{:S(2)}) copy-start(f32[2,64,2048]{2,1,0:T(8,128)} %param.10) | copy-start | bytes 3145732

commit v6 on v5

--- a/solution.py
+++ b/solution.py
@@ -286,7 +286,7 @@
             ys[v] = jnp.dot(t1[v], x1[v], preferred_element_type=F32)
             return c
 
-        lax.fori_loop(0, 4, first, 0, unroll=2)
+        lax.fori_loop(0, 4, first, 0, unroll=4)
 
         def butterfly(i):
             at = pl.multiple_of(i * 64, 64)
@@ -314,12 +314,12 @@
             got = jnp.dot(xq[q], t2[q], preferred_element_type=F32)
             re, im = got[:, :Q], got[:, Q:]
             factor = 1.0 - smq[q, pl.ds(e * 64, 64), :] * lax.rsqrt(jnp.maximum(re * re + im * im, 0.25))
-            rq[:, :Q] = (re * factor).astype(BF16)
-            rq[:, Q:] = (im * factor).astype(BF16)
-            zs[q] = jnp.dot(rq[...], t3[q], preferred_element_type=F32)
-            return c
-
-        lax.fori_loop(0, 4, field, 0)
+            rq[q & 1, :, :Q] = (re * factor).astype(BF16)
+            rq[q & 1, :, Q:] = (im * factor).astype(BF16)
+            zs[q] = jnp.dot(rq[q & 1], t3[q], preferred_element_type=F32)
+            return c
+
+        lax.fori_loop(0, 4, field, 0, unroll=2)
         def combine(i):
             lanes = pl.ds(pl.multiple_of(i * LANES, LANES), LANES)
             z0, z1, z2, z3 = (zs[q, :, lanes] for q in range(4))
@@ -362,7 +362,7 @@
             wo[pl.ds(q * 32, 32)] = swap(got).reshape(32, STRIPS, LANES)
             return c
 
-        lax.fori_loop(0, 4, last, 0, unroll=2)
+        lax.fori_loop(0, 4, last, 0, unroll=4)
 
         def pupil_sum(g, c):
             rows = pl.ds(pl.multiple_of(g * LANES, LANES), LANES)
@@ -414,7 +414,7 @@
                     src_ref=pg16.at[(led + i) & 3], dst_ref=rsr.at[led], send_sem=s5.at[i - 1], recv_sem=r5,
                     device_id=along(i), device_id_type=MESH,
                 ).start()
-        lax.fori_loop(0, 15, terms, 0)
+        lax.fori_loop(0, 15, terms, 0, unroll=3)
         term(15, True)
         pltpu.make_async_copy(send4.at[e, me], recv4.at[e, slot_me], r4.at[e]).start()
         if e == 0:
@@ -499,7 +499,7 @@
             pltpu.VMEM((PER, W, LANES), BF16),
             pltpu.VMEM((PER, BLOCKS, 64, LANES), BF16),
             pltpu.VMEM((4, 64, 2 * Q), BF16),
-            pltpu.VMEM((64, 2 * Q), BF16),
+            pltpu.VMEM((2, 64, 2 * Q), BF16),
             pltpu.VMEM((4, 64, 2 * Q), F32),
             pltpu.VMEM((PER, W, LANES), BF16),
             pltpu.VMEM((PER, BLOCKS, 64, LANES), BF16),

time: 89 us -> 88.6 us (level)
  no operation moved by 1% of the time
where the time goes in v6:
time: 88.6 us; the launch traced here: 88.4 us
  Pallas kernels  84.9 us (96%)
  local copies, waits for them, and re-layouts  2.88 us (3%)
    pallas_call x1, Pallas kernels, local(): pl.pallas_call(core_kernel, out_shape=(jax.ShapeDtypeStruct(EXCHANGE, BF1...  76.4 us
    pallas_call x1, Pallas kernels, local(): pl.pallas_call(add_kernel, out_shape=(jax.ShapeDtypeStruct(x.shape, F32),...  6.04 us
    unnamed x10, local copies, waits for them, and re-layouts  2.88 us
    pallas_call x1, Pallas kernels, local(): pl.pallas_call(cut_kernel, out_shape=jax.ShapeDtypeStruct(EXCHANGE, BF16)...  2.39 us

profile of v6, /device:TPU:0, one launch (start us, length us, event | category | flops | bytes accessed | tf_op | source)
XLA Modules:
  0.0 88.4 jit_solution(2007487368808738026)
XLA Ops:
  0.6 0.0 copy-start.4
  0.6 0.0 copy-start
  0.7 2.2 %copy-done = f32[1,64,2,8192]{3,2,1,0:T(2,128)S(1)} copy-done((f32[1,64,2,8192]{3,2,1,0:T(2,128)S(1)}, f32[1,64,2,8192]{3,2,1,0:T(2,128)}, u32[]{:S(2)}) %copy-start) | copy-done | bytes 4194328
  2.8 0.0 copy-start.3
  2.8 0.7 copy-done.3
  3.5 0.0 copy-start.1
  3.5 0.0 copy-start.2
  3.5 2.4 %cut.1.send1 = bf16[2,128,16,128]{3,2,1,0:T(8,128)(2,1)S(1)} custom-call(s32[2,8]{1,0:T(2,128)S(1)} %bitcast.21, f32[64,128,128]{2,1,0:T(8,128)S(1)} %bitcast.18), custom_call_target="tpu_custom_call" | custom-call | tf_op jit(solution)/shard_map/cut/pallas_call | solution.py:469
  5.9 0.0 copy-done.4
  5.9 0.0 copy-done.1
  5.9 0.0 copy-done.2
  5.9 76.4 %core.1 = (bf16[2,128,16,128]{3,2,1,0:T(8,128)(2,1)S(1)}, f32[128,2048]{1,0:T(8,128)S(1)}) custom-call(s32[2,8]{1,0:T(2,128)S(1)} %bitcast.22, bf16[2,128,16,128]{3,2,1,0:T(8,128)(2,1)S(1)} %cut.1.send1, f32[128,2048]{1,0:T(8,128)S(1)} %bitcast.19, f32[128,2048]{1,0:T(8,128)S(1)} %bitcast.20, bf16[4,512,1024]{2,1,0:T(8,128)(2,1)} %constant.8.clone.h1, ...), custom_call_target="tpu_custom_call" | custom-call | tf_op jit(solution)/shard_map/core/pallas_call | solution.py:479
  82.4 6.0 %add.1 = (f32[64,128,128]{2,1,0:T(8,128)}, f32[128,2048]{1,0:T(8,128)}) custom-call(s32[2,8]{1,0:T(2,128)S(1)} %bitcast.23, bf16[2,128,16,128]{3,2,1,0:T(8,128)(2,1)S(1)} %get-tuple-element.6.terms, f32[128,2048]{1,0:T(8,128)S(1)} %get-tuple-element.7.pgrad), custom_call_target="tpu_custom_call" | custom-call | tf_op jit(solution)/shard_map/add/pallas_call | solution.py:520
Async XLA Ops:
  0.6 5.3 %copy-start.4 = (s32[8,2]{0,1:T(2,128)S(1)}, s32[8,2]{0,1:T(2,128)}, u32[]{:S(2)}) copy-start(s32[8,2]{0,1:T(2,128)} %param.11) | copy-start | bytes 196
  0.6 2.2 %copy-start = (f32[1,64,2,8192]{3,2,1,0:T(2,128)S(1)}, f32[1,64,2,8192]{3,2,1,0:T(2,128)}, u32[]{:S(2)}) copy-start(f32[1,64,2,8192]{3,2,1,0:T(2,128)} %param.8) | copy-start | bytes 12582916
  2.8 0.7 copy-start.3
  3.5 2.4 %copy-start.1 = (f32[2,2048,64]{1,2,0:T(8,128)S(1)}, f32[2,2048,64]{1,2,0:T(8,128)}, u32[]{:S(2)}) copy-start(f32[2,2048,64]{1,2,0:T(8,128)} %param.9) | copy-start | bytes 3145732
  3.5 2.4 %copy-start.2 = (f32[2,64,2048]{2,1,0:T(8,128)S(1)}, f32[2,64,2048]{2,1,0:T(8,128)}, u32[]{:S(2)}) copy-start(f32[2,64,2048]{2,1,0:T(8,128)} %param.10) | copy-start | bytes 3145732

commit v7 on v6

--- a/solution.py
+++ b/solution.py
@@ -280,7 +280,7 @@
             x1[g >> 2, pl.ds(at + Q, LANES), :] = ((other * pr - win * pi) * sgn).astype(BF16)
             return c
 
-        lax.fori_loop(0, 16, product, 0, unroll=2)
+        lax.fori_loop(0, 16, product, 0, unroll=4)
 
         def first(v, c):
             ys[v] = jnp.dot(t1[v], x1[v], preferred_element_type=F32)

time: 88.6 us -> 88.3 us (level)
  no operation moved by 1% of the time
where the time goes in v7:
time: 88.3 us; the launch traced here: 88.2 us
  Pallas kernels  84.7 us (96%)
  local copies, waits for them, and re-layouts  2.88 us (3%)
    pallas_call x1, Pallas kernels, local(): pl.pallas_call(core_kernel, out_shape=(jax.ShapeDtypeStruct(EXCHANGE, BF1...  76.2 us
    pallas_call x1, Pallas kernels, local(): pl.pallas_call(add_kernel, out_shape=(jax.ShapeDtypeStruct(x.shape, F32),...  6.11 us
    unnamed x10, local copies, waits for them, and re-layouts  2.88 us
    pallas_call x1, Pallas kernels, local(): pl.pallas_call(cut_kernel, out_shape=jax.ShapeDtypeStruct(EXCHANGE, BF16)...  2.39 us

profile of v7, /device:TPU:0, one launch (start us, length us, event | category | flops | bytes accessed | tf_op | source)
XLA Modules:
  0.0 88.2 jit_solution(7838625199286741178)
XLA Ops:
  0.6 0.0 copy-start.4
  0.6 0.0 copy-start
  0.7 2.2 %copy-done = f32[1,64,2,8192]{3,2,1,0:T(2,128)S(1)} copy-done((f32[1,64,2,8192]{3,2,1,0:T(2,128)S(1)}, f32[1,64,2,8192]{3,2,1,0:T(2,128)}, u32[]{:S(2)}) %copy-start) | copy-done | bytes 4194328
  2.8 0.0 copy-start.3
  2.8 0.7 copy-done.3
  3.5 0.0 copy-start.1
  3.5 0.0 copy-start.2
  3.5 2.4 %cut.1.send1 = bf16[2,128,16,128]{3,2,1,0:T(8,128)(2,1)S(1)} custom-call(s32[2,8]{1,0:T(2,128)S(1)} %bitcast.21, f32[64,128,128]{2,1,0:T(8,128)S(1)} %bitcast.18), custom_call_target="tpu_custom_call" | custom-call | tf_op jit(solution)/shard_map/cut/pallas_call | solution.py:469
  5.9 0.0 copy-done.4
  5.9 0.0 copy-done.1
  5.9 0.0 copy-done.2
  5.9 76.2 %core.1 = (bf16[2,128,16,128]{3,2,1,0:T(8,128)(2,1)S(1)}, f32[128,2048]{1,0:T(8,128)S(1)}) custom-call(s32[2,8]{1,0:T(2,128)S(1)} %bitcast.22, bf16[2,128,16,128]{3,2,1,0:T(8,128)(2,1)S(1)} %cut.1.send1, f32[128,2048]{1,0:T(8,128)S(1)} %bitcast.19, f32[128,2048]{1,0:T(8,128)S(1)} %bitcast.20, bf16[4,512,1024]{2,1,0:T(8,128)(2,1)} %constant.8.clone.h1, ...), custom_call_target="tpu_custom_call" | custom-call | tf_op jit(solution)/shard_map/core/pallas_call | solution.py:479
  82.1 6.1 %add.1 = (f32[64,128,128]{2,1,0:T(8,128)}, f32[128,2048]{1,0:T(8,128)}) custom-call(s32[2,8]{1,0:T(2,128)S(1)} %bitcast.23, bf16[2,128,16,128]{3,2,1,0:T(8,128)(2,1)S(1)} %get-tuple-element.6.terms, f32[128,2048]{1,0:T(8,128)S(1)} %get-tuple-element.7.pgrad), custom_call_target="tpu_custom_call" | custom-call | tf_op jit(solution)/shard_map/add/pallas_call | solution.py:520
Async XLA Ops:
  0.6 5.3 %copy-start.4 = (s32[8,2]{0,1:T(2,128)S(1)}, s32[8,2]{0,1:T(2,128)}, u32[]{:S(2)}) copy-start(s32[8,2]{0,1:T(2,128)} %param.11) | copy-start | bytes 196
  0.6 2.2 %copy-start = (f32[1,64,2,8192]{3,2,1,0:T(2,128)S(1)}, f32[1,64,2,8192]{3,2,1,0:T(2,128)}, u32[]{:S(2)}) copy-start(f32[1,64,2,8192]{3,2,1,0:T(2,128)} %param.8) | copy-start | bytes 12582916
  2.8 0.7 copy-start.3
  3.5 2.4 %copy-start.1 = (f32[2,2048,64]{1,2,0:T(8,128)S(1)}, f32[2,2048,64]{1,2,0:T(8,128)}, u32[]{:S(2)}) copy-start(f32[2,2048,64]{1,2,0:T(8,128)} %param.9) | copy-start | bytes 3145732
  3.5 2.4 %copy-start.2 = (f32[2,64,2048]{2,1,0:T(8,128)S(1)}, f32[2,64,2048]{2,1,0:T(8,128)}, u32[]{:S(2)}) copy-start(f32[2,64,2048]{2,1,0:T(8,128)} %param.10) | copy-start | bytes 3145732
